TPU v7x, 32 devices: a whole 2x2x4 slice. The times are simulated.
32 devices in a mesh: mic: 8 (over y, x, core), proj: 4 (over z).
Axes of the slice: x: 2, y: 2, z: 4, core: 2. Of those that a mesh axis runs over, the one named last changes fastest.
Arguments:
- map_slabs: bfloat16 [20, 8, 256, 256], P('proj'), may hold values from -1.25 to 1.25
- slot_slab: int32 [20], P('proj'), may hold values from -1 to 11, as said below
- orient_index: int32 [4], replicated, may hold values from 0 to 255
- slab_lo: int32 [4], replicated, may hold values from 0 to 4
- slab_hi: int32 [4], replicated, may hold values from 8 to 12
- tile_spectrum: bfloat16 [32, 512, 1024], P(('mic', 'proj')), may hold values from -6 to 6
- prev_max: float32 [32, 512, 512], P(('mic', 'proj')), may hold values from -6 to 6
- prev_sum: float32 [32, 512, 512], P(('mic', 'proj')), may hold values from -12 to 12
- prev_sumsq: float32 [32, 512, 512], P(('mic', 'proj')), may hold values from 0.5 to 4
Outputs:
- best_score: float32 [32, 512, 512], P(('mic', 'proj'))
- score_sum: float32 [32, 512, 512], P(('mic', 'proj'))
- score_sumsq: float32 [32, 512, 512], P(('mic', 'proj'))
Inputs may be any that keep to these rules, and one draw needn't show every extreme that they name: `slot_slab`: each slab 0 to 11 stands in exactly one slot; every other slot holds -1. One index of proj holds 5 slabs; the others may hold fewer, and may hold none.
All inputs are finite; a program needn't handle non-finite values.
Results may differ from a plain program's by a relative error of at most 0.0057.
Values may be sent and summed in bfloat16 or wider, within the bound.
No kernel may reach another device: no remote copies, remote signals or barrier semaphores. Data moves between devices by JAX's collectives and lax.ppermute only.
A program may use at most 128 MiB of HBM per device.

v0:
```python
import math

import jax
import jax.numpy as jnp
from jax import lax
from jax.sharding import PartitionSpec as P

SLAB_Z = 8
SLABS = 12
NORI = 256


max_slope = 0.5
golden_angle = 2.399963


def matmul(left_op, right_op):
    return jnp.dot(left_op, right_op, preferred_element_type=jnp.float32)


def tent_weight(offsets):
    return jnp.maximum(0.0, 1.0 - jnp.abs(offsets))


def orient_slopes(orient_index):
    search_step = orient_index.astype(jnp.float32)
    radius = max_slope * jnp.sqrt((search_step + 0.5) / NORI)
    return (
        radius * jnp.cos(golden_angle * search_step),
        radius * jnp.sin(golden_angle * search_step),
    )


def phase_parts(freq_count, pixel_count, length):
    freqs = jnp.arange(freq_count, dtype=jnp.int32)[:, None]
    pixels = jnp.arange(pixel_count, dtype=jnp.int32)[None, :]
    turn_frac = (freqs * pixels % length).astype(jnp.float32) / length
    norm_scale = 1.0 / math.sqrt(length)
    return (
        jnp.cos(2.0 * math.pi * turn_frac) * norm_scale,
        jnp.sin(2.0 * math.pi * turn_frac) * norm_scale,
    )


def dft_tables(box_edge, tile_edge):
    row_cos, row_sin = phase_parts(box_edge, tile_edge, tile_edge)
    row_table = jnp.concatenate([row_cos, -row_sin], axis=1).astype(jnp.bfloat16)
    col_cos, col_sin = phase_parts(tile_edge, box_edge, tile_edge)
    column_table = jnp.concatenate([col_cos, -col_sin], axis=0).astype(jnp.bfloat16)
    full_cos, full_sin = phase_parts(tile_edge, tile_edge, tile_edge)
    inverse_table = jnp.concatenate([full_cos, full_sin], axis=1).astype(jnp.bfloat16)
    final_table = jnp.concatenate([full_cos, -full_sin], axis=1).astype(jnp.bfloat16)
    return (row_table, column_table, inverse_table, final_table)


def project(map_slabs, slot_slab, slab_lo, slab_hi, slope_x, slope_y, first_row, row_count):
    box_edge = map_slabs.shape[2]
    center = (SLABS * SLAB_Z - 1) / 2.0
    positions = jnp.arange(box_edge, dtype=jnp.int32).astype(jnp.float32)
    row_pos = (first_row + jnp.arange(row_count, dtype=jnp.int32)).astype(jnp.float32)
    within = jnp.arange(SLAB_Z, dtype=jnp.int32)
    projection = jnp.zeros((slope_x.shape[0], row_count, box_edge), jnp.float32)
    for slot_number in range(map_slabs.shape[0]):
        slab_id = slot_slab[slot_number]
        depths = (slab_id * SLAB_Z + within).astype(jnp.float32) - center
        shift_x = slope_x[:, None] * depths[None, :]
        shift_y = slope_y[:, None] * depths[None, :]
        left_tent = tent_weight(
            positions[None, None, None, :]
            - row_pos[None, None, :, None]
            - shift_x[:, :, None, None]
        ).astype(jnp.bfloat16)
        right_tent = tent_weight(
            positions[None, None, None, :]
            - positions[None, None, :, None]
            - shift_y[:, :, None, None]
        ).astype(jnp.bfloat16)
        sheared = jnp.einsum(
            "ojax,jxy->ojay", left_tent, map_slabs[slot_number], preferred_element_type=jnp.float32
        ).astype(jnp.bfloat16)
        slab_term = jnp.einsum(
            "ojay,ojby->oab", sheared, right_tent, preferred_element_type=jnp.float32
        )
        inside = ((slab_id >= slab_lo) & (slab_id < slab_hi)).astype(jnp.float32)
        projection = projection + inside[:, None, None] * slab_term
    return projection


def finish(real_part, imag_part, spectrum_tile, inverse_table, final_table):
    edge = spectrum_tile.shape[0]
    micro_real = spectrum_tile[:, :edge].astype(jnp.float32)
    micro_imag = spectrum_tile[:, edge:].astype(jnp.float32)
    product = jnp.concatenate(
        [
            micro_real * real_part + micro_imag * imag_part,
            micro_imag * real_part - micro_real * imag_part,
        ],
        axis=0,
    ).astype(jnp.bfloat16)
    halfway = matmul(product, inverse_table)
    half_real = halfway[:edge, :edge] - halfway[edge:, edge:]
    half_imag = halfway[:edge, edge:] + halfway[edge:, :edge]
    half_stack = jnp.concatenate([half_real, half_imag], axis=0).astype(jnp.bfloat16)
    return matmul(final_table, half_stack)


def correlate(row_block, spectrum_tile, column_table, inverse_table, final_table):
    edge = spectrum_tile.shape[0]
    stacked = matmul(column_table, row_block)
    real_part = stacked[:edge, :edge] - stacked[edge:, edge:]
    imag_part = stacked[:edge, edge:] + stacked[edge:, :edge]
    return finish(real_part, imag_part, spectrum_tile, inverse_table, final_table)


def body(
    map_slabs,
    slot_slab,
    orient_index,
    slab_lo,
    slab_hi,
    tile_spectrum,
    prev_max,
    prev_sum,
    prev_sumsq,
):
    box_edge = map_slabs.shape[2]
    tile_edge = tile_spectrum.shape[1]
    orient_count = orient_index.shape[0]
    row_count = box_edge // lax.axis_size("mic")
    first_row = lax.axis_index("mic") * row_count
    slope_x, slope_y = orient_slopes(orient_index)
    partial_value = project(
        map_slabs, slot_slab, slab_lo, slab_hi, slope_x, slope_y, first_row, row_count
    )
    row_table, column_table, inverse_table, final_table = dft_tables(box_edge, tile_edge)
    local_rows = lax.psum(partial_value, "proj").astype(jnp.bfloat16)
    local_rows = jnp.einsum(
        "oay,yk->oak", local_rows, row_table, preferred_element_type=jnp.float32
    ).astype(jnp.bfloat16)
    row_spectrum = lax.all_gather(local_rows, "mic", axis=1, tiled=True)
    spectrum_tile = tile_spectrum[0]

    def per_orient(orient, running):
        best_run, total_run, square_run = running
        row_block = lax.dynamic_index_in_dim(row_spectrum, orient, 0, keepdims=False)
        scores = correlate(row_block, spectrum_tile, column_table, inverse_table, final_table)
        return (jnp.maximum(best_run, scores), total_run + scores, square_run + scores * scores)

    best_score, score_sum, score_sumsq = lax.fori_loop(
        0, orient_count, per_orient, (prev_max[0], prev_sum[0], prev_sumsq[0])
    )
    return (best_score[None], score_sum[None], score_sumsq[None])


def solution(mesh):
    in_specs = (
        P("proj", None, None, None),
        P("proj"),
        P(),
        P(),
        P(),
        P(("mic", "proj"), None, None),
        P(("mic", "proj"), None, None),
        P(("mic", "proj"), None, None),
        P(("mic", "proj"), None, None),
    )
    out_specs = (
        P(("mic", "proj"), None, None),
        P(("mic", "proj"), None, None),
        P(("mic", "proj"), None, None),
    )
    return jax.shard_map(body, mesh=mesh, in_specs=in_specs, out_specs=out_specs, check_vma=False)
```

profile of v0, /device:TPU:0, one launch (start us, length us, event | category | flops | bytes accessed | tf_op | source)
XLA Modules:
  0.0 139.9 jit_solution(1051296424692873359)
XLA Ops:
  7.2 2.2 %negate_convert_fusion.2 = (bf16[256,512]{1,0:T(8,128)(2,1)S(1)}, bf16[256,512]{1,0:T(8,128)(2,1)S(1)}) fusion(), kind=kLoop, calls=%fused_computation.124 | loop fusion | flops 2490368 | bytes 524288 | tf_op jit(solution)/shard_map/convert.11
  9.4 1.4 %fusion.128 = (s32[1]{0:T(128)}, s32[1]{0:T(128)}, s32[1]{0:T(128)}, s32[1]{0:T(128)}, s32[1]{0:T(128)}) fusion(s32[5]{0:T(128)} %param.12), kind=kLoop, calls=%fused_computation.160 | loop fusion | bytes 40 | tf_op jit(solution)/shard_map/slice | solution.py:64
  14.0 0.7 cosine_multiply_fusion
  14.9 3.8 %and_convert_fusion = (f32[4]{0:T(128)S(1)}, f32[4]{0:T(128)S(1)}, f32[4]{0:T(128)S(1)}, f32[4]{0:T(128)S(1)}, f32[4]{0:T(128)S(1)}) fusion(s32[4]{0:T(128)} %param.15, s32[4]{0:T(128)} %param.14, s32[]{:T(128)} %bitcast.31, s32[]{:T(128)} %bitcast.19, s32[]{:T(128)} %bitcast.13, s32[]{:T(128)} %bitcast.7, s32[]{:T(128)} %bitcast.25), kind=kLoop, calls=%fused_computation.133 | loop fusion | flops 80 | bytes 132 | tf_op jit(solution)/shard_map/convert_element_type | solution.py:84
  18.8 9.3 %maximum_convert_fusion = (bf16[4,8,256,256]{3,2,1,0:T(8,128)(2,1)}, bf16[4,8,256,256]{3,2,1,0:T(8,128)(2,1)}, bf16[4,8,256,256]{3,2,1,0:T(8,128)(2,1)}, bf16[4,...) fusion(f32[4,8]{1,0:T(4,128)S(1)} %get-tuple-element.208, f32[256,256]{1,0:T(8,128)S(1)} %broadcast_subtract_fusion, ...), kind=kLoop, calls=%fused_computation.29 | loop fusion | flops 52428800 | bytes 21234304 | tf_op jit(solution)/shard_map/convert_element_type | solution.py:77
  28.1 0.8 maximum_convert_fusion.5
  29.0 4.0 %fusion.72 = f32[4,32,256]{2,1,0:T(8,128)S(1)} fusion(bf16[4,8,256,256]{3,2,1,0:T(8,128)(2,1)} %get-tuple-element.194, bf16[5,8,256,256]{3,2,1,0:T(8,128)(2,1)} %param.11, bf16[4,8,32,256]{3,2,1,0:T(8,128)(2,1)S(1)} %get-tuple-element.199, f32[4]{0:T(128)S(1)} %get-tuple-element.203), kind=kOutput, calls=%fused_computation.73 | convolution fusion | flops 268730368 | bytes 5898256 | tf_op jit(solution)/shard_map/ojay,ojby->oab/dot_general | solution.py:81
  33.0 4.0 %fusion.69 = f32[4,32,256]{2,1,0:T(8,128)S(1)} fusion(f32[4,32,256]{2,1,0:T(8,128)S(1)} %fusion.72, bf16[4,8,256,256]{3,2,1,0:T(8,128)(2,1)} %get-tuple-element.191, bf16[5,8,256,256]{3,2,1,0:T(8,128)(2,1)} %param.11, bf16[4,8,32,256]{3,2,1,0:T(8,128)(2,1)S(1)} %get-tuple-element.196, f32[4]{0:T(128)S(1)} %get-tuple-element.202), kind=kOutput, calls=%fused_computation.72 | convolution fusion | flops 268763136 | bytes 6029328 | tf_op jit(solution)/shard_map/ojay,ojby->oab/dot_general | solution.py:81
  37.0 4.0 %fusion.63 = f32[4,32,256]{2,1,0:T(8,128)S(1)} fusion(f32[4,32,256]{2,1,0:T(8,128)S(1)} %fusion.69, bf16[4,8,256,256]{3,2,1,0:T(8,128)(2,1)} %get-tuple-element.192, bf16[5,8,256,256]{3,2,1,0:T(8,128)(2,1)} %param.11, bf16[4,8,32,256]{3,2,1,0:T(8,128)(2,1)S(1)} %get-tuple-element.197, f32[4]{0:T(128)S(1)} %get-tuple-element.201), kind=kOutput, calls=%fused_computation.70 | convolution fusion | flops 268763136 | bytes 6029328 | tf_op jit(solution)/shard_map/ojay,ojby->oab/dot_general | solution.py:81
  41.0 4.0 %fusion.57 = f32[4,32,256]{2,1,0:T(8,128)S(1)} fusion(f32[4,32,256]{2,1,0:T(8,128)S(1)} %fusion.63, bf16[4,8,256,256]{3,2,1,0:T(8,128)(2,1)} %get-tuple-element.193, bf16[5,8,256,256]{3,2,1,0:T(8,128)(2,1)} %param.11, bf16[4,8,32,256]{3,2,1,0:T(8,128)(2,1)S(1)} %get-tuple-element.198, f32[4]{0:T(128)S(1)} %get-tuple-element.204), kind=kOutput, calls=%fused_computation.68 | convolution fusion | flops 268763136 | bytes 6029328 | tf_op jit(solution)/shard_map/ojay,ojby->oab/dot_general | solution.py:81
  45.1 4.1 %fusion.51 = f32[4,32,256]{2,1,0:T(8,128)S(1)} fusion(f32[4,32,256]{2,1,0:T(8,128)S(1)} %fusion.57, bf16[4,8,256,256]{3,2,1,0:T(8,128)(2,1)} %get-tuple-element.190, bf16[5,8,256,256]{3,2,1,0:T(8,128)(2,1)} %param.11, bf16[4,8,32,256]{3,2,1,0:T(8,128)(2,1)S(1)} %get-tuple-element.195, f32[4]{0:T(128)S(1)} %get-tuple-element.200), kind=kOutput, calls=%fused_computation.66 | convolution fusion | flops 268763136 | bytes 6029328 | tf_op jit(solution)/shard_map/ojay,ojby->oab/dot_general | solution.py:81
  49.2 23.3 %all-reduce.1 = bf16[4,32,256]{2,1,0:T(8,128)(2,1)S(1)} all-reduce(f32[4,32,256]{2,1,0:T(8,128)S(1)} %fusion.51), channel_id=1, replica_groups=mesh['mic'=8,'proj'=4] {'proj'}, use_global_device_ids=true, to_apply=%region_0.1 | all-reduce | flops 32768 | bytes 196608 | tf_op jit(solution)/shard_map/psum | solution.py:136
  72.5 0.9 convolution_convert_fusion.5
  73.8 1.6 %copy.13 = f32[1,512,512]{1,2,0:T(8,128)S(1)} copy(f32[1,512,512]{2,1,0:T(8,128)} %param.18) | data formatting | bytes 2097152 | tf_op args[7]
  75.3 1.6 %copy.14 = f32[1,512,512]{1,2,0:T(8,128)S(1)} copy(f32[1,512,512]{2,1,0:T(8,128)} %param.19) | data formatting | bytes 2097152 | tf_op args[8]
  76.9 4.0 %fusion.101 = bf16[512,512]{1,0:T(8,128)(2,1)S(1)} fusion(), kind=kLoop, calls=%fused_computation.98 | loop fusion | flops 4194304 | bytes 524288 | tf_op jit(solution)/shard_map/convert.7
  80.9 2.2 %negate_convert_fusion.1 = (bf16[512,256]{1,0:T(8,128)(2,1)S(1)}, bf16[512,256]{1,0:T(8,128)(2,1)S(1)}) fusion(), kind=kLoop, calls=%fused_computation.120 | loop fusion | flops 2490368 | bytes 524288 | tf_op jit(solution)/shard_map/convert.9
  83.1 0.8 pad_maximum_fusion.2
  83.9 4.4 %negate_convert_fusion = (bf16[512,512]{1,0:T(8,128)(2,1)S(1)}, bf16[512,512]{1,0:T(8,128)(2,1)S(1)}) fusion(), kind=kLoop, calls=%fused_computation.82 | loop fusion | flops 4980736 | bytes 1048576 | tf_op jit(solution)/shard_map/convert.5
  88.3 1.6 %pad_maximum_fusion = (bf16[512,1024]{1,0:T(8,128)(2,1)}, bf16[512,1024]{1,0:T(8,128)(2,1)}) fusion(bf16[512,512]{1,0:T(8,128)(2,1)S(1)} %get-tuple-element.231, bf16[512,512]{1,0:T(8,128)(2,1)S(1)} %get-tuple-element.230, bf16[512,512]{1,0:T(8,128)(2,1)S(1)} %fusion.101), kind=kLoop, calls=%fused_computation.58 | loop fusion | flops 3670016 | bytes 3670016 | tf_op jit(solution)/shard_map/concatenate | solution.py:52
  89.9 10.0 %all-gather.2.cloned.1.call-done = bf16[4,256,1024]{2,1,0:T(8,128)(2,1)} async-done(((bf16[4,32,1024]{2,1,0:T(8,128)(2,1)}), bf16[4,256,1024]{2,1,0:T(8,128)(2,1)}) %all-gather.2.cloned.1.call-update) | async-done | bytes 2097168 | tf_op jit(solution)/shard_map/all_gather | solution.py:140
  99.9 29.2 %while.17 = (s32[]{:T(128)}, f32[512,512]{0,1:T(8,128)S(1)}, f32[512,512]{0,1:T(8,128)S(1)}, f32[512,512]{0,1:T(8,128)S(1)}, bf16[512,1024]{1,0:T(8,128)(2,1)}, ...) while((s32[]{:T(128)}, f32[512,512]{0,1:T(8,128)S(1)}, ...), condition=%wide.region_2.3_spmd, body=%wide.region_1.2_spmd.sunk | while | flops 2156920832 | bytes 44040888 | solution.py:149
  99.9 2.0 %convolution_bitcast_fusion.3 = f32[1024,1024]{1,0:T(8,128)S(1)} fusion(bf16[1024,256]{1,0:T(8,128)(2,1)} %get-tuple-element.327, bf16[4,256,1024]{2,1,0:T(8,128)(2,1)} %get-tuple-element.326, s32[]{:T(128)} %get-tuple-element.311), kind=kOutput, calls=%fused_computation.clone.1 | convolution fusion | flops 536870912 | bytes 5243392 | tf_op jit(solution)/shard_map/while/body/eval_jaxpr/dot_general | solution.py:18
  102.0 0.7 fusion.146
  102.6 0.5 copy-done.2
  103.2 1.2 fusion.147
  104.8 0.8 copy-done
  105.7 1.6 %multiply_add_fusion.2 = (f32[512,512]{0,1:T(8,128)S(1)}, f32[512,512]{0,1:T(8,128)S(1)}, f32[512,512]{0,1:T(8,128)S(1)}) fusion(f32[512,512]{0,1:T(8,128)S(1)} %get-tuple-element.314, f32[512,512]{0,1:T(8,128)S(1)} %get-tuple-element.313, f32[512,512]{0,1:T(8,128)S(1)} %get-tuple-element.312, bf16[512,1024]{1,0:T(8,128)(2,1)S(1)} %copy-done, ...), kind=kOutput, calls=%fused_computation.23.clone.1 | convolution fusion | flops 540016640 | bytes 8388608 | tf_op jit(solution)/shard_map/while/body/eval_jaxpr/dot_general | solution.py:18
  107.2 2.0 %convolution_bitcast_fusion.3 = f32[1024,1024]{1,0:T(8,128)S(1)} fusion(bf16[1024,256]{1,0:T(8,128)(2,1)} %get-tuple-element.327, bf16[4,256,1024]{2,1,0:T(8,128)(2,1)} %get-tuple-element.326, s32[]{:T(128)} %get-tuple-element.311), kind=kOutput, calls=%fused_computation.clone.1 | convolution fusion | flops 536870912 | bytes 5243392 | tf_op jit(solution)/shard_map/while/body/eval_jaxpr/dot_general | solution.py:18
  109.3 0.7 fusion.146
  110.0 0.5 copy-done.2
  110.5 1.2 fusion.147
  112.1 0.8 copy-done
  113.0 1.6 %multiply_add_fusion.2 = (f32[512,512]{0,1:T(8,128)S(1)}, f32[512,512]{0,1:T(8,128)S(1)}, f32[512,512]{0,1:T(8,128)S(1)}) fusion(f32[512,512]{0,1:T(8,128)S(1)} %get-tuple-element.314, f32[512,512]{0,1:T(8,128)S(1)} %get-tuple-element.313, f32[512,512]{0,1:T(8,128)S(1)} %get-tuple-element.312, bf16[512,1024]{1,0:T(8,128)(2,1)S(1)} %copy-done, ...), kind=kOutput, calls=%fused_computation.23.clone.1 | convolution fusion | flops 540016640 | bytes 8388608 | tf_op jit(solution)/shard_map/while/body/eval_jaxpr/dot_general | solution.py:18
  114.6 2.0 %convolution_bitcast_fusion.3 = f32[1024,1024]{1,0:T(8,128)S(1)} fusion(bf16[1024,256]{1,0:T(8,128)(2,1)} %get-tuple-element.327, bf16[4,256,1024]{2,1,0:T(8,128)(2,1)} %get-tuple-element.326, s32[]{:T(128)} %get-tuple-element.311), kind=kOutput, calls=%fused_computation.clone.1 | convolution fusion | flops 536870912 | bytes 5243392 | tf_op jit(solution)/shard_map/while/body/eval_jaxpr/dot_general | solution.py:18
  116.6 0.7 fusion.146
  117.3 0.5 copy-done.2
  117.8 1.2 fusion.147
  119.4 0.8 copy-done
  120.3 1.6 %multiply_add_fusion.2 = (f32[512,512]{0,1:T(8,128)S(1)}, f32[512,512]{0,1:T(8,128)S(1)}, f32[512,512]{0,1:T(8,128)S(1)}) fusion(f32[512,512]{0,1:T(8,128)S(1)} %get-tuple-element.314, f32[512,512]{0,1:T(8,128)S(1)} %get-tuple-element.313, f32[512,512]{0,1:T(8,128)S(1)} %get-tuple-element.312, bf16[512,1024]{1,0:T(8,128)(2,1)S(1)} %copy-done, ...), kind=kOutput, calls=%fused_computation.23.clone.1 | convolution fusion | flops 540016640 | bytes 8388608 | tf_op jit(solution)/shard_map/while/body/eval_jaxpr/dot_general | solution.py:18
  121.9 2.0 %convolution_bitcast_fusion.3 = f32[1024,1024]{1,0:T(8,128)S(1)} fusion(bf16[1024,256]{1,0:T(8,128)(2,1)} %get-tuple-element.327, bf16[4,256,1024]{2,1,0:T(8,128)(2,1)} %get-tuple-element.326, s32[]{:T(128)} %get-tuple-element.311), kind=kOutput, calls=%fused_computation.clone.1 | convolution fusion | flops 536870912 | bytes 5243392 | tf_op jit(solution)/shard_map/while/body/eval_jaxpr/dot_general | solution.py:18
  123.9 0.7 fusion.146
  125.1 1.2 fusion.147
  126.7 0.8 copy-done
  127.6 1.6 %multiply_add_fusion.2 = (f32[512,512]{0,1:T(8,128)S(1)}, f32[512,512]{0,1:T(8,128)S(1)}, f32[512,512]{0,1:T(8,128)S(1)}) fusion(f32[512,512]{0,1:T(8,128)S(1)} %get-tuple-element.314, f32[512,512]{0,1:T(8,128)S(1)} %get-tuple-element.313, f32[512,512]{0,1:T(8,128)S(1)} %get-tuple-element.312, bf16[512,1024]{1,0:T(8,128)(2,1)S(1)} %copy-done, ...), kind=kOutput, calls=%fused_computation.23.clone.1 | convolution fusion | flops 540016640 | bytes 8388608 | tf_op jit(solution)/shard_map/while/body/eval_jaxpr/dot_general | solution.py:18
  129.2 1.3 copy.15
  130.5 1.3 copy.16
  131.8 1.3 copy.17
  (34 shorter events, 2.7 us)
Async XLA Ops:
  7.2 92.8 %all-gather.2.cloned.1.call-start = ((), (), s32[]{:S(2)}) async-start(), calls=%async_computation | async-start | bytes 2359296 | tf_op jit(solution)/shard_map/all_gather | solution.py:140
  45.1 28.4 %copy-start.3 = (f32[1,512,512]{2,1,0:T(8,128)S(1)}, f32[1,512,512]{2,1,0:T(8,128)}, u32[]{:S(2)}) copy-start(f32[1,512,512]{2,1,0:T(8,128)} %param.17) | copy-start | bytes 3145732
  99.9 2.0 %copy-start.1 = (bf16[512,1024]{1,0:T(8,128)(2,1)S(1)}, bf16[512,1024]{1,0:T(8,128)(2,1)}, u32[]{:S(2)}) copy-start(bf16[512,1024]{1,0:T(8,128)(2,1)} %get-tuple-element.325) | copy-start | bytes 3145732 | tf_op jit(solution)/shard_map/while
  101.9 1.2 copy-start.2
  104.4 1.2 copy-start
  107.2 2.0 %copy-start.1 = (bf16[512,1024]{1,0:T(8,128)(2,1)S(1)}, bf16[512,1024]{1,0:T(8,128)(2,1)}, u32[]{:S(2)}) copy-start(bf16[512,1024]{1,0:T(8,128)(2,1)} %get-tuple-element.325) | copy-start | bytes 3145732 | tf_op jit(solution)/shard_map/while
  109.2 1.2 copy-start.2
  111.7 1.2 copy-start
  114.5 2.0 %copy-start.1 = (bf16[512,1024]{1,0:T(8,128)(2,1)S(1)}, bf16[512,1024]{1,0:T(8,128)(2,1)}, u32[]{:S(2)}) copy-start(bf16[512,1024]{1,0:T(8,128)(2,1)} %get-tuple-element.325) | copy-start | bytes 3145732 | tf_op jit(solution)/shard_map/while
  116.6 1.2 copy-start.2
  119.0 1.2 copy-start
  121.9 2.0 %copy-start.1 = (bf16[512,1024]{1,0:T(8,128)(2,1)S(1)}, bf16[512,1024]{1,0:T(8,128)(2,1)}, u32[]{:S(2)}) copy-start(bf16[512,1024]{1,0:T(8,128)(2,1)} %get-tuple-element.325) | copy-start | bytes 3145732 | tf_op jit(solution)/shard_map/while
  123.9 1.2 copy-start.2
  126.3 1.2 copy-start
Sparse Core Ops, SparseCore 0:
  73.6 26.3 all-gather.1
where the time goes:
time: 141 us; the launch traced here: 140 us
  matrix products  40.3 us (29%)
  other arithmetic  34.3 us (24%)
  blocking collectives  23.3 us (17%)
  between operations  17.3 us (12%)
  local copies, waits for them, and re-layouts  14.3 us (10%)
  waiting for transfers between devices  10 us (7%)
    psum x1, blocking collectives, body(): local_rows = lax.psum(partial_value, 'proj').astype(jnp.bfloat16)  23.3 us
    dot_general x5, matrix products, project(): jnp.einsum('ojay,ojby->oab', sheared, right_tent, preferred_element_type=...  20.2 us
    dot_general x12, matrix products, matmul(): return jnp.dot(left_op, right_op, preferred_element_type=jnp.float32)  19.2 us
    another operation x12, other arithmetic  17 us
    all_gather x1, waiting for transfers between devices, body(): row_spectrum = lax.all_gather(local_rows, 'mic', axis=1, tiled=True)  10 us
    convert_element_type x1, other arithmetic, project(): right_tent = tent_weight(positions[None, None, None, :] - positions[None,...  9.32 us
    while x24, local copies, waits for them, and re-layouts  5.53 us
    while x3, local copies, waits for them, and re-layouts, body(): lax.fori_loop(0, orient_count, per_orient, (prev_max[0], prev_sum[0], pre...  3.92 us
  transfers between devices with their start and end apart: 1, of which 1 were waited for; matrix products, arithmetic and copies ran while one was open for 12% of the time, Pallas kernels for 0%

commit v1 on v0

v1 whole, which is shorter than its diff:
```python
import math

import jax
import jax.numpy as jnp
import ml_dtypes
import numpy as np
from jax import lax
from jax.experimental import pallas as pl
from jax.experimental.pallas import tpu as pltpu
from jax.sharding import PartitionSpec as P

SLAB_Z = 8
SLABS = 12
NORI = 256
MAX_SLOPE = 0.5
GOLDEN_ANGLE = 2.399963

F32 = jnp.float32
BF16 = jnp.bfloat16


def phase_tables(edge):
    index = np.arange(edge, dtype=np.int64)
    turn = (index[:, None] * index[None, :] % edge).astype(np.float64) / edge
    scale = 1.0 / math.sqrt(edge)
    cos = (np.cos(2.0 * np.pi * turn) * scale).astype(np.float32)
    sin = (np.sin(2.0 * np.pi * turn) * scale).astype(np.float32)
    return cos.astype(ml_dtypes.bfloat16), sin.astype(ml_dtypes.bfloat16)


def class_order(edge):
    return np.concatenate([np.arange(r, edge, 4) for r in range(4)])


def constants(box, edge):
    cos, sin = phase_tables(edge)
    quarter = edge // 4
    order = class_order(edge)
    cg, sg = cos[order, :box].T, sin[order, :box].T
    row = np.block([[cg, -sg], [-sg, -cg]])
    quad = []
    for r in range(4):
        c, s = cos[r::4, :quarter], sin[r::4, :quarter]
        quad.append(np.block([[c, s], [-s, c]]))
    quad = np.stack(quad)
    quad_t = np.ascontiguousarray(quad.transpose(0, 2, 1))
    pick = np.zeros((2 * edge, edge), np.float32)
    pick[np.arange(edge), order] = 1.0
    pick[edge + np.arange(edge), (-order) % edge] = 1.0
    pick_rows = pick.astype(ml_dtypes.bfloat16)
    pick_cols = np.concatenate([0.5 * pick[:edge].T, 0.5 * pick[edge:].T], axis=0).astype(ml_dtypes.bfloat16)
    return tuple(jnp.asarray(x) for x in (row, quad, quad_t, pick_rows, pick_cols))


def dot(a, b):
    return jnp.dot(a, b, preferred_element_type=F32)


def tent(offsets):
    return jnp.maximum(0.0, 1.0 - jnp.abs(offsets))


def project_kernel(rows, window, slot_ref, orient_ref, lo_ref, hi_ref, map_ref, out_ref, slabs, diff_x, diff_y, acc, sems):
    slots, depth, box = map_ref.shape[0], map_ref.shape[1], map_ref.shape[2]
    me = lax.axis_index("mic")
    orient = (me % 2) * 2 + (me // 2) % 2
    first = (me // 4) * rows
    base = jnp.clip(first - 32, 0, box - window)
    base = pl.multiple_of(base // 16 * 16, 16)

    def fetch(i):
        return pltpu.make_async_copy(map_ref.at[i, :, pl.ds(base, window), :], slabs.at[i], sems.at[i])

    for i in range(slots):
        fetch(i).start()

    step = jnp.full((8, 128), orient_ref[orient], jnp.int32).astype(F32)
    radius = MAX_SLOPE * jnp.sqrt((step + 0.5) / NORI)
    slope_x = jnp.max(radius * jnp.cos(GOLDEN_ANGLE * step))
    slope_y = jnp.max(radius * jnp.sin(GOLDEN_ANGLE * step))
    low, high = lo_ref[orient], hi_ref[orient]

    a = lax.broadcasted_iota(jnp.int32, (rows, window), 0)
    b = lax.broadcasted_iota(jnp.int32, (rows, window), 1)
    diff_x[...] = (b - a + (base - first)).astype(F32)
    d = lax.broadcasted_iota(jnp.int32, (box, box), 0)
    c = lax.broadcasted_iota(jnp.int32, (box, box), 1)
    diff_y[...] = (d - c).astype(F32)
    acc[...] = jnp.zeros_like(acc)

    for i in range(slots):
        fetch(i).wait()
        slab = slot_ref[i]

        @pl.when((slab >= low) & (slab < high))
        def _():
            total = None
            for j in range(depth):
                z = (slab * depth + j).astype(F32) - (SLABS * SLAB_Z - 1) / 2.0
                left = tent(diff_x[...] - slope_x * z).astype(BF16)
                sheared = dot(left, slabs[i, j]).astype(BF16)
                right = tent(diff_y[...] - slope_y * z).astype(BF16)
                term = dot(sheared, right)
                total = term if total is None else total + term
            acc[...] += total

    out_ref[...] = acc[...].astype(BF16)


def project(map_slabs, slot_slab, orient_index, slab_lo, slab_hi, rows):
    slots, depth, box = map_slabs.shape[:3]
    blocks = box // rows
    window = min(box, rows + 32 * min(2, blocks - 1))
    smem = pl.BlockSpec(memory_space=pltpu.SMEM)
    return pl.pallas_call(
        lambda *refs: project_kernel(rows, window, *refs),
        out_shape=jax.ShapeDtypeStruct((rows, box), BF16),
        in_specs=[smem, smem, smem, smem, pl.BlockSpec(memory_space=pltpu.HBM)],
        out_specs=pl.BlockSpec(memory_space=pltpu.VMEM),
        scratch_shapes=[
            pltpu.VMEM((slots, depth, window, box), BF16),
            pltpu.VMEM((rows, window), F32),
            pltpu.VMEM((box, box), F32),
            pltpu.VMEM((rows, box), F32),
            pltpu.SemaphoreType.DMA((slots,)),
        ],
        compiler_params=pltpu.CompilerParams(vmem_limit_bytes=32 << 20),
        name="project",
    )(slot_slab, orient_index, slab_lo, slab_hi, map_slabs)


def hermitian_kernel(tile_ref, rows_ref, cols_ref, real_ref, imag_ref, picked):
    edge = real_ref.shape[0]
    picked[...] = dot(rows_ref[...], tile_ref[...]).astype(BF16)
    real = jnp.concatenate([picked[:edge, :edge], picked[edge:, :edge]], axis=1)
    real_ref[...] = dot(real, cols_ref[...])
    imag = jnp.concatenate([picked[:edge, edge:], -picked[edge:, edge:]], axis=1)
    imag_ref[...] = dot(imag, cols_ref[...])


def hermitian(tile, pick_rows, pick_cols):
    edge = tile.shape[0]
    vmem = pl.BlockSpec(memory_space=pltpu.VMEM)
    return pl.pallas_call(
        hermitian_kernel,
        out_shape=[jax.ShapeDtypeStruct((edge, edge), F32)] * 2,
        in_specs=[vmem] * 3,
        out_specs=[vmem] * 2,
        scratch_shapes=[pltpu.VMEM((2 * edge, 2 * edge), BF16)],
        compiler_params=pltpu.CompilerParams(vmem_limit_bytes=32 << 20),
        cost_estimate=pl.CostEstimate(flops=8 * edge**3 * 2, bytes_accessed=12 * edge * edge, transcendentals=0),
        name="hermitian",
    )(tile, pick_rows, pick_cols)


def half_transform(pieces_ref, real_ref, imag_ref, row_ref, quad_ref, quadt_ref, stack, half):
    count, rows, box = pieces_ref.shape
    edge = real_ref.shape[0]
    quarter = edge // 4
    for q in range(count):
        stack[(q // 2) * rows : (q // 2 + 1) * rows, (q % 2) * box : (q % 2 + 1) * box] = pieces_ref[q]
    width = 2 * quarter
    for gh in range(edge // width):
        cols = slice(gh * width, (gh + 1) * width)
        rr = dot(stack[...], row_ref[:, gh * width : (gh + 1) * width])
        ri = dot(stack[...], row_ref[:, edge + gh * width : edge + (gh + 1) * width])
        r0, r1 = rr[:quarter], rr[quarter:]
        i0, i1 = ri[:quarter], ri[quarter:]
        inputs = ((r0 + r1, i0 + i1), (r0 + i1, i0 - r1), (r0 - r1, i0 - i1), (r0 - i1, i0 + r1))
        parts = []
        for r in range(4):
            u = jnp.concatenate(inputs[r], axis=0).astype(BF16)
            spec = dot(quad_ref[r], u)
            sr, si = spec[:quarter], spec[quarter:]
            fr = slice(r * quarter, (r + 1) * quarter)
            tr, ti = real_ref[fr, cols], imag_ref[fr, cols]
            product = jnp.concatenate([tr * sr + ti * si, ti * sr - tr * si], axis=0).astype(BF16)
            parts.append(dot(quadt_ref[r], product))
        ar, ai = parts[0][:quarter] + parts[2][:quarter], parts[0][quarter:] + parts[2][quarter:]
        br, bi = parts[0][:quarter] - parts[2][:quarter], parts[0][quarter:] - parts[2][quarter:]
        cr, ci = parts[1][:quarter] + parts[3][:quarter], parts[1][quarter:] + parts[3][quarter:]
        dr, di = parts[1][:quarter] - parts[3][:quarter], parts[1][quarter:] - parts[3][quarter:]
        outs = ((ar + cr, ai + ci), (br - di, bi + dr), (ar - cr, ai - ci), (br + di, bi - dr))
        for k in range(4):
            xs = slice(k * quarter, (k + 1) * quarter)
            hr, hi = outs[k][0].astype(BF16), outs[k][1].astype(BF16)
            for t in range(2):
                lanes = slice(t * quarter, (t + 1) * quarter)
                start = (2 * gh + t) * width
                half[xs, start : start + quarter] = hr[:, lanes]
                half[xs, start + quarter : start + width] = hi[:, lanes]


def first_kernel(pieces_ref, real_ref, imag_ref, row_ref, quad_ref, quadt_ref, half_ref, stack):
    half_transform(pieces_ref, real_ref, imag_ref, row_ref, quad_ref, quadt_ref, stack, half_ref)


def first_pair(pieces, th_real, th_imag, row, quad, quad_t):
    box, edge = pieces.shape[2], th_real.shape[0]
    vmem = pl.BlockSpec(memory_space=pltpu.VMEM)
    return pl.pallas_call(
        first_kernel,
        out_shape=jax.ShapeDtypeStruct((edge, 2 * edge), BF16),
        in_specs=[vmem] * 6,
        out_specs=vmem,
        scratch_shapes=[pltpu.VMEM((box, 2 * box), BF16)],
        compiler_params=pltpu.CompilerParams(vmem_limit_bytes=40 << 20),
        cost_estimate=pl.CostEstimate(flops=6 * edge**3, bytes_accessed=12 * edge * edge, transcendentals=0),
        name="first_pair",
    )(pieces, th_real, th_imag, row, quad, quad_t)


def scores_of(half, quad_ref, quarter):
    width = 2 * quarter
    f = [dot(half[:, s * width : (s + 1) * width], quad_ref[s]) for s in range(4)]
    re = [x[:, :quarter] for x in f]
    im = [x[:, quarter:] for x in f]
    ar, ai, br, bi = re[0] + re[2], im[0] + im[2], re[0] - re[2], im[0] - im[2]
    cr, ci, dr, di = re[1] + re[3], im[1] + im[3], re[1] - re[3], im[1] - im[3]
    return ((ar + cr, ai + ci), (br - di, bi + dr), (ar - cr, ai - ci), (br + di, bi - dr))


def second_kernel(
    pieces_ref, half_ref, real_ref, imag_ref, row_ref, quad_ref, quadt_ref, max_ref, sum_ref, sq_ref,
    best_ref, total_ref, square_ref, stack, other,
):
    block = max_ref.shape[1]
    quarter = max_ref.shape[2] // 4
    step = pl.program_id(0)

    @pl.when(step == 0)
    def _():
        half_transform(pieces_ref, real_ref, imag_ref, row_ref, quad_ref, quadt_ref, stack, other)

    xs = pl.ds(pl.multiple_of(step * block, block), block)
    one = scores_of(half_ref[xs, :], quad_ref, quarter)
    two = scores_of(other[xs, :], quad_ref, quarter)
    for k in range(4):
        ys = slice(k * quarter, (k + 1) * quarter)
        best, total, square = max_ref[0, :, ys], sum_ref[0, :, ys], sq_ref[0, :, ys]
        for score in (*one[k], *two[k]):
            best = jnp.maximum(best, score)
            total = total + score
            square = square + score * score
        best_ref[0, :, ys] = best
        total_ref[0, :, ys] = total
        square_ref[0, :, ys] = square


def second_pair(pieces, half, th_real, th_imag, row, quad, quad_t, prev_max, prev_sum, prev_sumsq):
    box, edge = pieces.shape[2], th_real.shape[0]
    block = edge // 4

    def whole(x):
        return pl.BlockSpec(x.shape, lambda i, n=x.ndim: (0,) * n)

    stat = pl.BlockSpec((1, block, edge), lambda i: (0, i, 0))
    return pl.pallas_call(
        second_kernel,
        grid=(edge // block,),
        out_shape=[jax.ShapeDtypeStruct(prev_max.shape, F32)] * 3,
        in_specs=[whole(x) for x in (pieces, half, th_real, th_imag, row, quad, quad_t)] + [stat] * 3,
        out_specs=[stat] * 3,
        scratch_shapes=[pltpu.VMEM((box, 2 * box), BF16), pltpu.VMEM((edge, 2 * edge), BF16)],
        compiler_params=pltpu.CompilerParams(vmem_limit_bytes=48 << 20),
        cost_estimate=pl.CostEstimate(flops=10 * edge**3, bytes_accessed=40 * edge * edge, transcendentals=0),
        name="second_pair",
    )(pieces, half, th_real, th_imag, row, quad, quad_t, prev_max, prev_sum, prev_sumsq)


def swap(value, axis, offset):
    return lax.ppermute(value, axis, [(i, i ^ offset) for i in range(lax.axis_size(axis))])


def gather_group(value, low_bit, bits):
    mine = (lax.axis_index("mic") >> low_bit) & ((1 << bits) - 1)
    got = [(k, swap(value, "mic", k << low_bit)) for k in range(1, 1 << bits)]
    out = jnp.zeros((1 << bits,) + value.shape, value.dtype)
    for k, block in [(0, value)] + got:
        out = lax.dynamic_update_index_in_dim(out, block, mine ^ k, 0)
    return out.reshape((-1,) + value.shape[1:])


def body(map_slabs, slot_slab, orient_index, slab_lo, slab_hi, tile_spectrum, prev_max, prev_sum, prev_sumsq):
    box, edge = map_slabs.shape[2], tile_spectrum.shape[1]
    devices = lax.axis_size("mic")
    bits = devices.bit_length() - 1
    rows = box * 4 // devices
    row, quad, quad_t, pick_rows, pick_cols = constants(box, edge)

    part = project(map_slabs, slot_slab, orient_index, slab_lo, slab_hi, rows)
    got = [swap(part, "proj", k) for k in range(1, lax.axis_size("proj"))]
    th_real, th_imag = hermitian(tile_spectrum[0], pick_rows, pick_cols)
    total = part.astype(F32)
    for block in got:
        total = total + block.astype(F32)
    pieces = total.astype(BF16)[None]
    for low in range(1, bits, 2):
        pieces = gather_group(pieces, low, min(2, bits - low))
    others = swap(pieces, "mic", 1)
    half = first_pair(pieces, th_real, th_imag, row, quad, quad_t)
    return tuple(second_pair(others, half, th_real, th_imag, row, quad, quad_t, prev_max, prev_sum, prev_sumsq))


def solution(mesh):
    tiles = P(("mic", "proj"), None, None)
    in_specs = (P("proj", None, None, None), P("proj"), P(), P(), P(), tiles, tiles, tiles, tiles)
    return jax.shard_map(body, mesh=mesh, in_specs=in_specs, out_specs=(tiles,) * 3, check_vma=False)
```

time: 141 us -> 42.9 us (0.30)
  matrix products: 40.3 us -> 0 us
  other arithmetic: 34.3 us -> 0.95 us
  blocking collectives: 23.3 us -> 0 us
  between operations: 17.3 us -> 0.77 us
  Pallas kernels: 0 us -> 13.1 us
  starting transfers between devices: 0.04 us -> 10.3 us
  local copies, waits for them, and re-layouts: 14.3 us -> 8.24 us
    dot_general x18 -> x0, matrix products: 40.3 us -> none  [the longest x5 20.2 us: project(): jnp.einsum('ojay,ojby->oab', sheared, right_tent, preferred_element_type=...]
    psum x1 -> x0, blocking collectives: 23.3 us -> none  [body(): local_rows = lax.psum(partial_value, 'proj').astype(jnp.bfloat16)]
    another operation x12 -> x0, other arithmetic: 17 us -> none
    convert_element_type x5 -> x0, other arithmetic: 14 us -> none  [the longest x1 9.32 us: project(): right_tent = tent_weight(positions[None, None, None, :] - positions[None,...]
    pallas_call x0 -> x4, Pallas kernels: none -> 13.1 us  [the longest x1 6.64 us: second_pair(): pl.pallas_call(second_kernel, grid=(edge // block,), out_shape=[jax.Shape...]
    ppermute x0 -> x7, starting transfers between devices: none -> 10.3 us  [swap(): lax.ppermute(value, axis, [(i, i ^ offset) for i in range(lax.axis_size(a...]
    all_gather x1 -> x0, waiting for transfers between devices: 10 us -> none  [body(): row_spectrum = lax.all_gather(local_rows, 'mic', axis=1, tiled=True)]
    while x27 -> x0, local copies, waits for them, and re-layouts: 9.44 us -> none
  transfers between devices with their start and end apart: 1 -> 7, of which waited for: 1 -> 5; matrix products, arithmetic and copies ran while one was open for 12% -> 0% of each run, Pallas kernels for 0% -> 10%
where the time goes in v1:
time: 42.9 us; the launch traced here: 42.4 us
  Pallas kernels  13.1 us (31%)
  starting transfers between devices  10.3 us (24%)
  waiting for transfers between devices  9.03 us (21%)
  local copies, waits for them, and re-layouts  8.24 us (19%)
  other arithmetic  0.95 us (2%)
  between operations  0.77 us (2%)
    ppermute x7, starting transfers between devices, swap(): lax.ppermute(value, axis, [(i, i ^ offset) for i in range(lax.axis_size(a...  10.3 us
    ppermute x7, waiting for transfers between devices, swap(): lax.ppermute(value, axis, [(i, i ^ offset) for i in range(lax.axis_size(a...  9.03 us
    unnamed x26, local copies, waits for them, and re-layouts  8.2 us
    pallas_call x1, Pallas kernels, second_pair(): pl.pallas_call(second_kernel, grid=(edge // block,), out_shape=[jax.Shape...  6.64 us
    pallas_call x1, Pallas kernels, project(): pl.pallas_call(lambda *refs: project_kernel(rows, window, *refs), out_sha...  2.41 us
    pallas_call x1, Pallas kernels, hermitian(): pl.pallas_call(hermitian_kernel, out_shape=[jax.ShapeDtypeStruct((edge, e...  2.33 us
    pallas_call x1, Pallas kernels, first_pair(): pl.pallas_call(first_kernel, out_shape=jax.ShapeDtypeStruct((edge, 2 * ed...  1.72 us
    dynamic_update_slice x1, other arithmetic, gather_group(): out = lax.dynamic_update_index_in_dim(out, block, mine ^ k, 0)  0.95 us
  transfers between devices with their start and end apart: 7, of which 5 were waited for; matrix products, arithmetic and copies ran while one was open for 0% of the time, Pallas kernels for 10%

profile of v1, /device:TPU:0, one launch (start us, length us, event | category | flops | bytes accessed | tf_op | source)
XLA Modules:
  0.0 42.4 jit_solution(12421734967978918859)
XLA Ops:
  0.6 0.0 copy-start
  0.6 2.5 %copy-done = bf16[5,8,256,256]{3,2,1,0:T(8,128)(2,1)S(1)} copy-done((bf16[5,8,256,256]{3,2,1,0:T(8,128)(2,1)S(1)}, bf16[5,8,256,256]{3,2,1,0:T(8,128)(2,1)}, u32[]{:S(2)}) %copy-start) | copy-done | bytes 5242904
  3.1 0.0 copy-start.4
  3.1 0.7 %copy-done.4 = s32[5]{0:T(128)S(1)} copy-done((s32[5]{0:T(128)S(1)}, s32[5]{0:T(128)}, u32[]{:S(2)}) %copy-start.4) | copy-done | bytes 44
  3.8 0.0 copy-start.5
  3.8 0.7 %copy-done.5 = s32[4]{0:T(128)S(1)} copy-done((s32[4]{0:T(128)S(1)}, s32[4]{0:T(128)}, u32[]{:S(2)}) %copy-start.5) | copy-done | bytes 40
  4.4 0.0 copy-start.6
  4.4 0.7 %copy-done.6 = s32[4]{0:T(128)S(1)} copy-done((s32[4]{0:T(128)S(1)}, s32[4]{0:T(128)}, u32[]{:S(2)}) %copy-start.6) | copy-done | bytes 40
  5.1 0.0 copy-start.7
  5.1 0.7 %copy-done.7 = s32[4]{0:T(128)S(1)} copy-done((s32[4]{0:T(128)S(1)}, s32[4]{0:T(128)}, u32[]{:S(2)}) %copy-start.7) | copy-done | bytes 40
  5.7 0.0 copy-start.8
  5.7 2.4 %project.1 = bf16[128,256]{1,0:T(8,128)(2,1)S(1)} custom-call(s32[5]{0:T(128)S(1)} %copy-done.4, s32[4]{0:T(128)S(1)} %copy-done.5, s32[4]{0:T(128)S(1)} %copy-done.6, s32[4]{0:T(128)S(1)} %copy-done.7, bf16[5,8,256,256]{3,2,1,0:T(8,128)(2,1)S(1)} %copy-done), custom_call_target="tpu_custom_call" | custom-call | tf_op jit(solution)/shard_map/project/pallas_call | solution.py:115
  8.2 0.0 copy-start.1
  8.2 0.0 copy-start.2
  8.2 0.0 copy-start.3
  8.2 5.8 %collective-permute-start.2 = (bf16[128,256]{1,0:T(8,128)(2,1)S(1)}, bf16[128,256]{1,0:T(8,128)(2,1)S(1)}, u32[]{:S(2)}, u32[]{:S(2)}) collective-permute-start(bf16[128,256]{1,0:T(8,128)(2,1)S(1)} %project.1), channel_id=1, source_target_pairs={{0,3},{1,2},{2,1},{3,0},{4,7},{5,6},{6,5},{7,4},{8,11},{9,10},{10,... | collective-permute-start | bytes 196616 | tf_op jit(solution)/shard_map/ppermute | solution.py:272
  14.0 0.4 collective-permute-start.1
  14.4 0.5 %collective-permute-start = (bf16[128,256]{1,0:T(8,128)(2,1)S(1)}, bf16[128,256]{1,0:T(8,128)(2,1)}, u32[]{:S(2)}, u32[]{:S(2)}) collective-permute-start(bf16[128,256]{1,0:T(8,128)(2,1)S(1)} %project.1), channel_id=1, source_target_pairs={{0,1},{1,0},{2,3},{3,2},{4,5},{5,4},{6,7},{7,6},{8,9},{9,8},{10,11... | collective-permute-start | bytes 196616 | tf_op jit(solution)/shard_map/ppermute | solution.py:272
  14.9 1.5 %collective-permute-done.2 = bf16[128,256]{1,0:T(8,128)(2,1)S(1)} collective-permute-done((bf16[128,256]{1,0:T(8,128)(2,1)S(1)}, bf16[128,256]{1,0:T(8,128)(2,1)S(1)}, u32[]{:S(2)}, u32[]{:S(2)}) %collective-permute-start.2) | collective-permute-done | bytes 65568 | tf_op jit(solution)/shard_map/ppermute | solution.py:272
  16.4 0.0 copy-start.11
  16.4 3.5 %collective-permute-done.1 = bf16[128,256]{1,0:T(8,128)(2,1)S(1)} collective-permute-done((bf16[128,256]{1,0:T(8,128)(2,1)S(1)}, bf16[128,256]{1,0:T(8,128)(2,1)S(1)}, u32[]{:S(2)}, u32[]{:S(2)}) %collective-permute-start.1) | collective-permute-done | bytes 65568 | tf_op jit(solution)/shard_map/ppermute | solution.py:272
  19.9 0.0 copy-done.11
  19.9 0.0 copy-start.12
  19.9 0.6 %copy-done.12 = bf16[128,256]{1,0:T(8,128)(2,1)} copy-done((bf16[128,256]{1,0:T(8,128)(2,1)}, bf16[128,256]{1,0:T(8,128)(2,1)S(1)}, u32[]{:S(2)}) %copy-start.12) | copy-done | bytes 65560
  20.6 0.0 collective-permute-done
  20.6 0.9 %constant_dynamic-update-slice_fusion.3 = (bf16[4,128,256]{2,1,0:T(8,128)(2,1)S(1)}, bf16[1,128,256]{2,1,0:T(8,128)(2,1)S(1)}) fusion(bf16[4,128,256]{2,1,0:T(8,128)(2,1)S(1)} %reshape.24, s32[]{:T(128)S(6)} %select_n.13, bf16[128,256]{1,0:T(8,128)(2,1)} %copy-done.11, bf16[128,256]{1,0:T(8,128)(2,1)} %copy-done.12, ...), kind=kLoop, calls=%fused_computation.5 | loop fusion | flops 262144 | bytes 393220 | tf_op jit(solution)/shard_map/jit(dynamic_update_index_in_dim)/dynamic_update_slice | solution.py:280
  21.5 0.9 %collective-permute-start.3 = (bf16[1,128,256]{2,1,0:T(8,128)(2,1)S(1)}, bf16[1,128,256]{2,1,0:T(8,128)(2,1)S(1)}, u32[]{:S(2)}, u32[]{:S(2)}) collective-permute-start(bf16[1,128,256]{2,1,0:T(8,128)(2,1)S(1)} %get-tuple-element.8), channel_id=1, source_target_pairs={{0,8},{4,12},{8,0},{12,4},{16,24},{20,28},{24,16},{28,20},{1,9},{5... | collective-permute-start | bytes 196616 | tf_op jit(solution)/shard_map/ppermute | solution.py:272
  22.4 1.5 %collective-permute-start.4 = (bf16[1,128,256]{2,1,0:T(8,128)(2,1)S(1)}, bf16[1,128,256]{2,1,0:T(8,128)(2,1)S(1)}, u32[]{:S(2)}, u32[]{:S(2)}) collective-permute-start(bf16[1,128,256]{2,1,0:T(8,128)(2,1)S(1)} %get-tuple-element.8), channel_id=1, source_target_pairs={{0,16},{4,20},{8,24},{12,28},{16,0},{20,4},{24,8},{28,12},{1,17},{... | collective-permute-start | bytes 196616 | tf_op jit(solution)/shard_map/ppermute | solution.py:272
  23.9 1.1 %collective-permute-start.5 = (bf16[1,128,256]{2,1,0:T(8,128)(2,1)S(1)}, bf16[1,128,256]{2,1,0:T(8,128)(2,1)S(1)}, u32[]{:S(2)}, u32[]{:S(2)}) collective-permute-start(bf16[1,128,256]{2,1,0:T(8,128)(2,1)S(1)} %get-tuple-element.8), channel_id=1, source_target_pairs={{0,24},{4,28},{8,16},{12,20},{16,8},{20,12},{24,0},{28,4},{1,25},{... | collective-permute-start | bytes 196616 | tf_op jit(solution)/shard_map/ppermute | solution.py:272
  25.1 0.8 %collective-permute-done.3 = bf16[1,128,256]{2,1,0:T(8,128)(2,1)S(1)} collective-permute-done((bf16[1,128,256]{2,1,0:T(8,128)(2,1)S(1)}, bf16[1,128,256]{2,1,0:T(8,128)(2,1)S(1)}, u32[]{:S(2)}, u32[]{:S(2)}) %collective-permute-start.3) | collective-permute-done | bytes 65568 | tf_op jit(solution)/shard_map/ppermute | solution.py:272
  25.9 0.8 %collective-permute-done.4 = bf16[1,128,256]{2,1,0:T(8,128)(2,1)S(1)} collective-permute-done((bf16[1,128,256]{2,1,0:T(8,128)(2,1)S(1)}, bf16[1,128,256]{2,1,0:T(8,128)(2,1)S(1)}, u32[]{:S(2)}, u32[]{:S(2)}) %collective-permute-start.4) | collective-permute-done | bytes 65568 | tf_op jit(solution)/shard_map/ppermute | solution.py:272
  26.7 2.4 %collective-permute-done.5 = bf16[1,128,256]{2,1,0:T(8,128)(2,1)S(1)} collective-permute-done((bf16[1,128,256]{2,1,0:T(8,128)(2,1)S(1)}, bf16[1,128,256]{2,1,0:T(8,128)(2,1)S(1)}, u32[]{:S(2)}, u32[]{:S(2)}) %collective-permute-start.5) | collective-permute-done | bytes 65568 | tf_op jit(solution)/shard_map/ppermute | solution.py:272
  29.1 0.1 collective-permute-start.6
  29.2 0.0 copy-done.8
  29.2 0.0 copy-start.9
  29.2 1.2 %copy-done.9 = bf16[1024,512]{1,0:T(8,128)(2,1)S(1)} copy-done((bf16[1024,512]{1,0:T(8,128)(2,1)S(1)}, bf16[1024,512]{1,0:T(8,128)(2,1)}, u32[]{:S(2)}) %copy-start.9) | copy-done | bytes 1048600
  30.4 0.0 copy-start.10
  30.4 1.2 %copy-done.10 = bf16[1024,512]{1,0:T(8,128)(2,1)S(1)} copy-done((bf16[1024,512]{1,0:T(8,128)(2,1)S(1)}, bf16[1024,512]{1,0:T(8,128)(2,1)}, u32[]{:S(2)}) %copy-start.10) | copy-done | bytes 1048600
  31.7 2.3 %hermitian.1 = (f32[512,512]{1,0:T(8,128)S(1)}, f32[512,512]{1,0:T(8,128)S(1)}) custom-call(bf16[512,1024]{1,0:T(8,128)(2,1)S(1)} %bitcast.4, bf16[1024,512]{1,0:T(8,128)(2,1)S(1)} %copy-done.10, bf16[1024,512]{1,0:T(8,128)(2,1)S(1)} %copy-done.9), custom_call_target="tpu_custom_call" | custom-call | flops 2147483648 | bytes 3145728 | tf_op jit(solution)/shard_map/hermitian/pallas_call | solution.py:144
  34.0 0.0 copy-done.1
  34.0 0.0 copy-done.2
  34.0 0.0 copy-done.3
  34.0 1.7 %first_pair.1.half_ref = bf16[512,1024]{1,0:T(8,128)(2,1)S(1)} custom-call(bf16[4,128,256]{2,1,0:T(8,128)(2,1)S(1)} %constant_dynamic-update-slice_fusion.pieces_ref, f32[512,512]{1,0:T(8,128)S(1)} %get-tuple-element.5.real_ref, f32[512,512]{1,0:T(8,128)S(1)} %get-tuple-element.6.imag_ref, bf16[512,1024]{1,0:T(8,128)(2,1)S(1)} %copy-done.1, ...), custom_call_target="tpu_custom_call" | custom-call | flops 805306368 | bytes 3145728 | tf_op jit(solution)/shard_map/first_pair/pallas_call | solution.py:201
  35.8 0.0 collective-permute-done.6.pieces_ref
  35.8 6.6 %second_pair.1 = (f32[1,512,512]{2,1,0:T(8,128)}, f32[1,512,512]{2,1,0:T(8,128)}, f32[1,512,512]{2,1,0:T(8,128)}) custom-call(bf16[4,128,256]{2,1,0:T(8,128)(2,1)S(1)} %collective-permute-done.6.pieces_ref, bf16[512,1024]{1,0:T(8,128)(2,1)S(1)} %first_pair.1.half_ref, f32[512,512]{1,0:T(8,128)S(1)} %get-tuple-element.5.real_ref, ...), custom_call_target="tpu_custom_call" | custom-call | flops 1342177280 | bytes 10485760 | tf_op jit(solution)/shard_map/second_pair/pallas_call | solution.py:258
  (4 shorter events, 0.0 us)
Async XLA Ops:
  0.6 2.5 %copy-start = (bf16[5,8,256,256]{3,2,1,0:T(8,128)(2,1)S(1)}, bf16[5,8,256,256]{3,2,1,0:T(8,128)(2,1)}, u32[]{:S(2)}) copy-start(bf16[5,8,256,256]{3,2,1,0:T(8,128)(2,1)} %refs_4_.1) | copy-start | bytes 15728644
  3.1 0.7 %copy-start.4 = (s32[5]{0:T(128)S(1)}, s32[5]{0:T(128)}, u32[]{:S(2)}) copy-start(s32[5]{0:T(128)} %refs_0_.1) | copy-start | bytes 64
  3.8 0.7 %copy-start.5 = (s32[4]{0:T(128)S(1)}, s32[4]{0:T(128)}, u32[]{:S(2)}) copy-start(s32[4]{0:T(128)} %refs_1_.1) | copy-start | bytes 52
  4.4 0.7 %copy-start.6 = (s32[4]{0:T(128)S(1)}, s32[4]{0:T(128)}, u32[]{:S(2)}) copy-start(s32[4]{0:T(128)} %refs_2_.1) | copy-start | bytes 52
  5.1 0.7 %copy-start.7 = (s32[4]{0:T(128)S(1)}, s32[4]{0:T(128)}, u32[]{:S(2)}) copy-start(s32[4]{0:T(128)} %refs_3_.1) | copy-start | bytes 52
  5.7 23.5 %copy-start.8 = (bf16[1,512,1024]{2,1,0:T(8,128)(2,1)S(1)}, bf16[1,512,1024]{2,1,0:T(8,128)(2,1)}, u32[]{:S(2)}) copy-start(bf16[1,512,1024]{2,1,0:T(8,128)(2,1)} %param.19) | copy-start | bytes 3145732
  8.2 25.8 %copy-start.1 = (bf16[512,1024]{1,0:T(8,128)(2,1)S(1)}, bf16[512,1024]{1,0:T(8,128)(2,1)}, u32[]{:S(2)}) copy-start(bf16[512,1024]{1,0:T(8,128)(2,1)} %constant.40.clone.row_ref) | copy-start | bytes 3145732
  8.2 25.8 %copy-start.2 = (bf16[4,256,256]{2,1,0:T(8,128)(2,1)S(1)}, bf16[4,256,256]{2,1,0:T(8,128)(2,1)}, u32[]{:S(2)}) copy-start(bf16[4,256,256]{2,1,0:T(8,128)(2,1)} %constant.42.clone.quadt_ref) | copy-start | bytes 1572868
  8.2 25.8 %copy-start.3 = (bf16[4,256,256]{2,1,0:T(8,128)(2,1)S(1)}, bf16[4,256,256]{2,1,0:T(8,128)(2,1)}, u32[]{:S(2)}) copy-start(bf16[4,256,256]{2,1,0:T(8,128)(2,1)} %constant.41.clone.quad_ref) | copy-start | bytes 1572868
  8.2 8.2 %collective-permute-start.2 = (bf16[128,256]{1,0:T(8,128)(2,1)S(1)}, bf16[128,256]{1,0:T(8,128)(2,1)S(1)}, u32[]{:S(2)}, u32[]{:S(2)}) collective-permute-start(bf16[128,256]{1,0:T(8,128)(2,1)S(1)} %project.1), channel_id=1, source_target_pairs={{0,3},{1,2},{2,1},{3,0},{4,7},{5,6},{6,5},{7,4},{8,11},{9,10},{10,... | collective-permute-start | bytes 196616 | tf_op jit(solution)/shard_map/ppermute | solution.py:272
  14.0 5.9 %collective-permute-start.1 = (bf16[128,256]{1,0:T(8,128)(2,1)S(1)}, bf16[128,256]{1,0:T(8,128)(2,1)S(1)}, u32[]{:S(2)}, u32[]{:S(2)}) collective-permute-start(bf16[128,256]{1,0:T(8,128)(2,1)S(1)} %project.1), channel_id=1, source_target_pairs={{0,2},{1,3},{2,0},{3,1},{4,6},{5,7},{6,4},{7,5},{8,10},{9,11},{10,... | collective-permute-start | bytes 196616 | tf_op jit(solution)/shard_map/ppermute | solution.py:272
  14.4 6.2 %collective-permute-start = (bf16[128,256]{1,0:T(8,128)(2,1)S(1)}, bf16[128,256]{1,0:T(8,128)(2,1)}, u32[]{:S(2)}, u32[]{:S(2)}) collective-permute-start(bf16[128,256]{1,0:T(8,128)(2,1)S(1)} %project.1), channel_id=1, source_target_pairs={{0,1},{1,0},{2,3},{3,2},{4,5},{5,4},{6,7},{7,6},{8,9},{9,8},{10,11... | collective-permute-start | bytes 196616 | tf_op jit(solution)/shard_map/ppermute | solution.py:272
  16.4 3.5 %copy-start.11 = (bf16[128,256]{1,0:T(8,128)(2,1)}, bf16[128,256]{1,0:T(8,128)(2,1)S(1)}, u32[]{:S(2)}) copy-start(bf16[128,256]{1,0:T(8,128)(2,1)S(1)} %collective-permute-done.2) | copy-start | bytes 196612
  19.9 0.6 %copy-start.12 = (bf16[128,256]{1,0:T(8,128)(2,1)}, bf16[128,256]{1,0:T(8,128)(2,1)S(1)}, u32[]{:S(2)}) copy-start(bf16[128,256]{1,0:T(8,128)(2,1)S(1)} %collective-permute-done.1) | copy-start | bytes 196612
  21.5 4.3 %collective-permute-start.3 = (bf16[1,128,256]{2,1,0:T(8,128)(2,1)S(1)}, bf16[1,128,256]{2,1,0:T(8,128)(2,1)S(1)}, u32[]{:S(2)}, u32[]{:S(2)}) collective-permute-start(bf16[1,128,256]{2,1,0:T(8,128)(2,1)S(1)} %get-tuple-element.8), channel_id=1, source_target_pairs={{0,8},{4,12},{8,0},{12,4},{16,24},{20,28},{24,16},{28,20},{1,9},{5... | collective-permute-start | bytes 196616 | tf_op jit(solution)/shard_map/ppermute | solution.py:272
  22.4 4.3 %collective-permute-start.4 = (bf16[1,128,256]{2,1,0:T(8,128)(2,1)S(1)}, bf16[1,128,256]{2,1,0:T(8,128)(2,1)S(1)}, u32[]{:S(2)}, u32[]{:S(2)}) collective-permute-start(bf16[1,128,256]{2,1,0:T(8,128)(2,1)S(1)} %get-tuple-element.8), channel_id=1, source_target_pairs={{0,16},{4,20},{8,24},{12,28},{16,0},{20,4},{24,8},{28,12},{1,17},{... | collective-permute-start | bytes 196616 | tf_op jit(solution)/shard_map/ppermute | solution.py:272
  23.9 5.2 %collective-permute-start.5 = (bf16[1,128,256]{2,1,0:T(8,128)(2,1)S(1)}, bf16[1,128,256]{2,1,0:T(8,128)(2,1)S(1)}, u32[]{:S(2)}, u32[]{:S(2)}) collective-permute-start(bf16[1,128,256]{2,1,0:T(8,128)(2,1)S(1)} %get-tuple-element.8), channel_id=1, source_target_pairs={{0,24},{4,28},{8,16},{12,20},{16,8},{20,12},{24,0},{28,4},{1,25},{... | collective-permute-start | bytes 196616 | tf_op jit(solution)/shard_map/ppermute | solution.py:272
  29.1 6.6 %collective-permute-start.6 = (bf16[4,128,256]{2,1,0:T(8,128)(2,1)S(1)}, bf16[4,128,256]{2,1,0:T(8,128)(2,1)S(1)}, u32[]{:S(2)}, u32[]{:S(2)}) collective-permute-start(bf16[4,128,256]{2,1,0:T(8,128)(2,1)S(1)} %constant_dynamic-update-slice_fusion.pieces_ref), channel_id=1, source_target_pairs={{0,4},{4,0},{8,12},{12,8},{16,20},{20,16},{24,28},{28,24},{1,5},{5... | collective-permute-start | bytes 786440 | tf_op jit(solution)/shard_map/ppermute | solution.py:272
  29.2 1.2 %copy-start.9 = (bf16[1024,512]{1,0:T(8,128)(2,1)S(1)}, bf16[1024,512]{1,0:T(8,128)(2,1)}, u32[]{:S(2)}) copy-start(bf16[1024,512]{1,0:T(8,128)(2,1)} %constant.44.clone.cols_ref) | copy-start | bytes 3145732
  30.4 1.2 %copy-start.10 = (bf16[1024,512]{1,0:T(8,128)(2,1)S(1)}, bf16[1024,512]{1,0:T(8,128)(2,1)}, u32[]{:S(2)}) copy-start(bf16[1024,512]{1,0:T(8,128)(2,1)} %constant.43.clone.rows_ref) | copy-start | bytes 3145732

commit v2 on v1

--- a/solution.py
+++ b/solution.py
@@ -17,6 +17,7 @@
 
 F32 = jnp.float32
 BF16 = jnp.bfloat16
+TAP = jnp.int16
 
 
 def phase_tables(edge):
@@ -44,12 +45,7 @@
         quad.append(np.block([[c, s], [-s, c]]))
     quad = np.stack(quad)
     quad_t = np.ascontiguousarray(quad.transpose(0, 2, 1))
-    pick = np.zeros((2 * edge, edge), np.float32)
-    pick[np.arange(edge), order] = 1.0
-    pick[edge + np.arange(edge), (-order) % edge] = 1.0
-    pick_rows = pick.astype(ml_dtypes.bfloat16)
-    pick_cols = np.concatenate([0.5 * pick[:edge].T, 0.5 * pick[edge:].T], axis=0).astype(ml_dtypes.bfloat16)
-    return tuple(jnp.asarray(x) for x in (row, quad, quad_t, pick_rows, pick_cols))
+    return tuple(jnp.asarray(x) for x in (row, quad, quad_t))
 
 
 def dot(a, b):
@@ -60,7 +56,21 @@
     return jnp.maximum(0.0, 1.0 - jnp.abs(offsets))
 
 
-def project_kernel(rows, window, slot_ref, orient_ref, lo_ref, hi_ref, map_ref, out_ref, slabs, diff_x, diff_y, acc, sems):
+def two_taps(index, shift):
+    whole = jnp.floor(shift)
+    frac = shift - whole
+    tap = whole.astype(jnp.int32)
+    tap, next_tap = tap.astype(index.dtype), (tap + 1).astype(index.dtype)
+    low = jnp.full(index.shape, 1.0 - frac, F32).astype(BF16)
+    high = jnp.full(index.shape, frac, F32).astype(BF16)
+    zero = jnp.zeros(index.shape, BF16)
+    return jnp.where(index == tap, low, jnp.where(index == next_tap, high, zero))
+
+
+def project_kernel(
+    rows, window, slot_hbm, orient_hbm, lo_hbm, hi_hbm, map_ref, out_ref,
+    slabs, diff_x, diff_y, sheared, right, acc, sems, slot_ref, orient_ref, lo_ref, hi_ref, param_sems,
+):
     slots, depth, box = map_ref.shape[0], map_ref.shape[1], map_ref.shape[2]
     me = lax.axis_index("mic")
     orient = (me % 2) * 2 + (me // 2) % 2
@@ -71,9 +81,17 @@
     def fetch(i):
         return pltpu.make_async_copy(map_ref.at[i, :, pl.ds(base, window), :], slabs.at[i], sems.at[i])
 
+    params = [
+        pltpu.make_async_copy(src, dst, param_sems.at[n])
+        for n, (src, dst) in enumerate(((slot_hbm, slot_ref), (orient_hbm, orient_ref), (lo_hbm, lo_ref), (hi_hbm, hi_ref)))
+    ]
+    for copy in params:
+        copy.start()
     for i in range(slots):
         fetch(i).start()
 
+    for copy in params:
+        copy.wait()
     step = jnp.full((8, 128), orient_ref[orient], jnp.int32).astype(F32)
     radius = MAX_SLOPE * jnp.sqrt((step + 0.5) / NORI)
     slope_x = jnp.max(radius * jnp.cos(GOLDEN_ANGLE * step))
@@ -82,11 +100,14 @@
 
     a = lax.broadcasted_iota(jnp.int32, (rows, window), 0)
     b = lax.broadcasted_iota(jnp.int32, (rows, window), 1)
-    diff_x[...] = (b - a + (base - first)).astype(F32)
+    diff_x[...] = (b - a + (base - first)).astype(diff_x.dtype)
     d = lax.broadcasted_iota(jnp.int32, (box, box), 0)
     c = lax.broadcasted_iota(jnp.int32, (box, box), 1)
-    diff_y[...] = (d - c).astype(F32)
+    diff_y[...] = (d - c).astype(diff_y.dtype)
     acc[...] = jnp.zeros_like(acc)
+    right[...] = jnp.zeros_like(right)
+    half = box // 2
+    bands = ((slice(0, half + 32), slice(0, half)), (slice(half - 32, box), slice(half, box)))
 
     for i in range(slots):
         fetch(i).wait()
@@ -94,15 +115,13 @@
 
         @pl.when((slab >= low) & (slab < high))
         def _():
-            total = None
             for j in range(depth):
                 z = (slab * depth + j).astype(F32) - (SLABS * SLAB_Z - 1) / 2.0
-                left = tent(diff_x[...] - slope_x * z).astype(BF16)
-                sheared = dot(left, slabs[i, j]).astype(BF16)
-                right = tent(diff_y[...] - slope_y * z).astype(BF16)
-                term = dot(sheared, right)
-                total = term if total is None else total + term
-            acc[...] += total
+                left = two_taps(diff_x[...], slope_x * z)
+                sheared[:, j * box : (j + 1) * box] = dot(left, slabs[i, j]).astype(BF16)
+                for ds, cs in bands:
+                    right[j * box + ds.start : j * box + ds.stop, cs] = two_taps(diff_y[ds, cs], slope_y * z)
+            acc[...] += dot(sheared[...], right[...])
 
     out_ref[...] = acc[...].astype(BF16)
 
@@ -111,46 +130,86 @@
     slots, depth, box = map_slabs.shape[:3]
     blocks = box // rows
     window = min(box, rows + 32 * min(2, blocks - 1))
-    smem = pl.BlockSpec(memory_space=pltpu.SMEM)
+    args = [pltpu.with_memory_space_constraint(x, pltpu.HBM) for x in (slot_slab, orient_index, slab_lo, slab_hi, map_slabs)]
     return pl.pallas_call(
         lambda *refs: project_kernel(rows, window, *refs),
         out_shape=jax.ShapeDtypeStruct((rows, box), BF16),
-        in_specs=[smem, smem, smem, smem, pl.BlockSpec(memory_space=pltpu.HBM)],
+        in_specs=[pl.BlockSpec(memory_space=pltpu.HBM)] * 5,
         out_specs=pl.BlockSpec(memory_space=pltpu.VMEM),
         scratch_shapes=[
             pltpu.VMEM((slots, depth, window, box), BF16),
-            pltpu.VMEM((rows, window), F32),
-            pltpu.VMEM((box, box), F32),
+            pltpu.VMEM((rows, window), TAP),
+            pltpu.VMEM((box, box), TAP),
+            pltpu.VMEM((rows, depth * box), BF16),
+            pltpu.VMEM((depth * box, box), BF16),
             pltpu.VMEM((rows, box), F32),
             pltpu.SemaphoreType.DMA((slots,)),
+            pltpu.SMEM(slot_slab.shape, jnp.int32),
+            pltpu.SMEM(orient_index.shape, jnp.int32),
+            pltpu.SMEM(orient_index.shape, jnp.int32),
+            pltpu.SMEM(orient_index.shape, jnp.int32),
+            pltpu.SemaphoreType.DMA((4,)),
         ],
-        compiler_params=pltpu.CompilerParams(vmem_limit_bytes=32 << 20),
+        compiler_params=pltpu.CompilerParams(vmem_limit_bytes=16 << 20),
         name="project",
-    )(slot_slab, orient_index, slab_lo, slab_hi, map_slabs)
-
-
-def hermitian_kernel(tile_ref, rows_ref, cols_ref, real_ref, imag_ref, picked):
+    )(*args)
+
+
+def total_kernel(*refs):
+    total = refs[0][...].astype(F32)
+    for ref in refs[1:-1]:
+        total = total + ref[...].astype(F32)
+    refs[-1][...] = total.astype(BF16)
+
+
+def total_of(parts):
+    vmem = pl.BlockSpec(memory_space=pltpu.VMEM)
+    return pl.pallas_call(
+        total_kernel,
+        out_shape=jax.ShapeDtypeStruct(parts[0].shape, BF16),
+        in_specs=[vmem] * len(parts),
+        out_specs=vmem,
+        compiler_params=pltpu.CompilerParams(vmem_limit_bytes=2 << 20),
+        name="total",
+    )(*parts)
+
+
+def hermitian_kernel(tile_ref, real_ref, imag_ref, picked):
     edge = real_ref.shape[0]
-    picked[...] = dot(rows_ref[...], tile_ref[...]).astype(BF16)
+    quarter = edge // 4
+
+    def pick(dim):
+        shape = (2 * edge, edge) if dim == 0 else (edge, 2 * edge)
+        place = lax.broadcasted_iota(jnp.int32, shape, dim)
+        freq = lax.broadcasted_iota(jnp.int32, shape, 1 - dim)
+        inner = place & (edge - 1)
+        wanted = 4 * (inner & (quarter - 1)) + inner // quarter
+        wanted = jnp.where(place < edge, wanted, (edge - wanted) & (edge - 1))
+        return freq == wanted
+
+    rows = jnp.where(pick(0), 1.0, 0.0).astype(BF16)
+    picked[...] = dot(rows, tile_ref[...]).astype(BF16)
+    cols = jnp.where(pick(1), 0.5, 0.0).astype(BF16)
+    cols = jnp.concatenate([cols[:, :edge], cols[:, edge:]], axis=0)
     real = jnp.concatenate([picked[:edge, :edge], picked[edge:, :edge]], axis=1)
-    real_ref[...] = dot(real, cols_ref[...])
+    real_ref[...] = dot(real, cols)
     imag = jnp.concatenate([picked[:edge, edge:], -picked[edge:, edge:]], axis=1)
-    imag_ref[...] = dot(imag, cols_ref[...])
-
-
-def hermitian(tile, pick_rows, pick_cols):
+    imag_ref[...] = dot(imag, cols)
+
+
+def hermitian(tile):
     edge = tile.shape[0]
     vmem = pl.BlockSpec(memory_space=pltpu.VMEM)
     return pl.pallas_call(
         hermitian_kernel,
         out_shape=[jax.ShapeDtypeStruct((edge, edge), F32)] * 2,
-        in_specs=[vmem] * 3,
+        in_specs=[vmem],
         out_specs=[vmem] * 2,
         scratch_shapes=[pltpu.VMEM((2 * edge, 2 * edge), BF16)],
-        compiler_params=pltpu.CompilerParams(vmem_limit_bytes=32 << 20),
+        compiler_params=pltpu.CompilerParams(vmem_limit_bytes=16 << 20),
         cost_estimate=pl.CostEstimate(flops=8 * edge**3 * 2, bytes_accessed=12 * edge * edge, transcendentals=0),
         name="hermitian",
-    )(tile, pick_rows, pick_cols)
+    )(tile)
 
 
 def half_transform(pieces_ref, real_ref, imag_ref, row_ref, quad_ref, quadt_ref, stack, half):
@@ -204,7 +263,7 @@
         in_specs=[vmem] * 6,
         out_specs=vmem,
         scratch_shapes=[pltpu.VMEM((box, 2 * box), BF16)],
-        compiler_params=pltpu.CompilerParams(vmem_limit_bytes=40 << 20),
+        compiler_params=pltpu.CompilerParams(vmem_limit_bytes=12 << 20),
         cost_estimate=pl.CostEstimate(flops=6 * edge**3, bytes_accessed=12 * edge * edge, transcendentals=0),
         name="first_pair",
     )(pieces, th_real, th_imag, row, quad, quad_t)
@@ -221,48 +280,53 @@
 
 
 def second_kernel(
-    pieces_ref, half_ref, real_ref, imag_ref, row_ref, quad_ref, quadt_ref, max_ref, sum_ref, sq_ref,
-    best_ref, total_ref, square_ref, stack, other,
+    block, pieces_ref, half_ref, real_ref, imag_ref, row_ref, quad_ref, quadt_ref, max_ref, sum_ref, sq_ref,
+    best_ref, total_ref, square_ref, stack, other, best_out, total_out, square_out, sems,
 ):
-    block = max_ref.shape[1]
-    quarter = max_ref.shape[2] // 4
-    step = pl.program_id(0)
-
-    @pl.when(step == 0)
-    def _():
-        half_transform(pieces_ref, real_ref, imag_ref, row_ref, quad_ref, quadt_ref, stack, other)
-
-    xs = pl.ds(pl.multiple_of(step * block, block), block)
-    one = scores_of(half_ref[xs, :], quad_ref, quarter)
-    two = scores_of(other[xs, :], quad_ref, quarter)
-    for k in range(4):
-        ys = slice(k * quarter, (k + 1) * quarter)
-        best, total, square = max_ref[0, :, ys], sum_ref[0, :, ys], sq_ref[0, :, ys]
-        for score in (*one[k], *two[k]):
-            best = jnp.maximum(best, score)
-            total = total + score
-            square = square + score * score
-        best_ref[0, :, ys] = best
-        total_ref[0, :, ys] = total
-        square_ref[0, :, ys] = square
+    edge = max_ref.shape[2]
+    quarter = edge // 4
+    half_transform(pieces_ref, real_ref, imag_ref, row_ref, quad_ref, quadt_ref, stack, other)
+    copies = []
+    for step in range(edge // block):
+        xs = slice(step * block, (step + 1) * block)
+        one = scores_of(half_ref[xs, :], quad_ref, quarter)
+        two = scores_of(other[xs, :], quad_ref, quarter)
+        for k in range(4):
+            ys = slice(k * quarter, (k + 1) * quarter)
+            best, total, square = max_ref[0, xs, ys], sum_ref[0, xs, ys], sq_ref[0, xs, ys]
+            for score in (*one[k], *two[k]):
+                best = jnp.maximum(best, score)
+                total = total + score
+                square = square + score * score
+            best_out[xs, ys] = best
+            total_out[xs, ys] = total
+            square_out[xs, ys] = square
+        for n, (src, dst) in enumerate(((best_out, best_ref), (total_out, total_ref), (square_out, square_ref))):
+            copy = pltpu.make_async_copy(src.at[xs, :], dst.at[0, xs, :], sems.at[step, n])
+            copy.start()
+            copies.append(copy)
+    for copy in copies:
+        copy.wait()
 
 
 def second_pair(pieces, half, th_real, th_imag, row, quad, quad_t, prev_max, prev_sum, prev_sumsq):
     box, edge = pieces.shape[2], th_real.shape[0]
     block = edge // 4
-
-    def whole(x):
-        return pl.BlockSpec(x.shape, lambda i, n=x.ndim: (0,) * n)
-
-    stat = pl.BlockSpec((1, block, edge), lambda i: (0, i, 0))
-    return pl.pallas_call(
-        second_kernel,
-        grid=(edge // block,),
+    vmem = pl.BlockSpec(memory_space=pltpu.VMEM)
+    return pl.pallas_call(
+        lambda *refs: second_kernel(block, *refs),
         out_shape=[jax.ShapeDtypeStruct(prev_max.shape, F32)] * 3,
-        in_specs=[whole(x) for x in (pieces, half, th_real, th_imag, row, quad, quad_t)] + [stat] * 3,
-        out_specs=[stat] * 3,
-        scratch_shapes=[pltpu.VMEM((box, 2 * box), BF16), pltpu.VMEM((edge, 2 * edge), BF16)],
-        compiler_params=pltpu.CompilerParams(vmem_limit_bytes=48 << 20),
+        in_specs=[vmem] * 10,
+        out_specs=[pl.BlockSpec(memory_space=pltpu.HBM)] * 3,
+        scratch_shapes=[
+            pltpu.VMEM((box, 2 * box), BF16),
+            pltpu.VMEM((edge, 2 * edge), BF16),
+            pltpu.VMEM((edge, edge), F32),
+            pltpu.VMEM((edge, edge), F32),
+            pltpu.VMEM((edge, edge), F32),
+            pltpu.SemaphoreType.DMA((edge // block, 3)),
+        ],
+        compiler_params=pltpu.CompilerParams(vmem_limit_bytes=16 << 20),
         cost_estimate=pl.CostEstimate(flops=10 * edge**3, bytes_accessed=40 * edge * edge, transcendentals=0),
         name="second_pair",
     )(pieces, half, th_real, th_imag, row, quad, quad_t, prev_max, prev_sum, prev_sumsq)
@@ -272,12 +336,23 @@
     return lax.ppermute(value, axis, [(i, i ^ offset) for i in range(lax.axis_size(axis))])
 
 
+def assemble_kernel(low_bit, bits, *refs):
+    mine = (lax.axis_index("mic") >> low_bit) & ((1 << bits) - 1)
+    for k, ref in enumerate(refs[:-1]):
+        refs[-1][mine ^ k] = ref[...]
+
+
 def gather_group(value, low_bit, bits):
-    mine = (lax.axis_index("mic") >> low_bit) & ((1 << bits) - 1)
-    got = [(k, swap(value, "mic", k << low_bit)) for k in range(1, 1 << bits)]
-    out = jnp.zeros((1 << bits,) + value.shape, value.dtype)
-    for k, block in [(0, value)] + got:
-        out = lax.dynamic_update_index_in_dim(out, block, mine ^ k, 0)
+    got = [swap(value, "mic", k << low_bit) for k in range(1, 1 << bits)]
+    vmem = pl.BlockSpec(memory_space=pltpu.VMEM)
+    out = pl.pallas_call(
+        lambda *refs: assemble_kernel(low_bit, bits, *refs),
+        out_shape=jax.ShapeDtypeStruct((1 << bits,) + value.shape, value.dtype),
+        in_specs=[vmem] * (1 << bits),
+        out_specs=vmem,
+        compiler_params=pltpu.CompilerParams(vmem_limit_bytes=4 << 20),
+        name="assemble",
+    )(value, *got)
     return out.reshape((-1,) + value.shape[1:])
 
 
@@ -286,15 +361,14 @@
     devices = lax.axis_size("mic")
     bits = devices.bit_length() - 1
     rows = box * 4 // devices
-    row, quad, quad_t, pick_rows, pick_cols = constants(box, edge)
+    row, quad, quad_t = constants(box, edge)
 
     part = project(map_slabs, slot_slab, orient_index, slab_lo, slab_hi, rows)
     got = [swap(part, "proj", k) for k in range(1, lax.axis_size("proj"))]
-    th_real, th_imag = hermitian(tile_spectrum[0], pick_rows, pick_cols)
-    total = part.astype(F32)
-    for block in got:
-        total = total + block.astype(F32)
-    pieces = total.astype(BF16)[None]
+    tile, _ = lax.optimization_barrier((tile_spectrum[0], part))
+    th_real, th_imag = hermitian(tile)
+    got, th_real, th_imag = lax.optimization_barrier((got, th_real, th_imag))
+    pieces = total_of([part] + got)[None]
     for low in range(1, bits, 2):
         pieces = gather_group(pieces, low, min(2, bits - low))
     others = swap(pieces, "mic", 1)

time: 42.9 us -> 27.7 us (0.65)
  local copies, waits for them, and re-layouts: 8.24 us -> 0.04 us
  waiting for transfers between devices: 9.03 us -> 6.59 us
  Pallas kernels: 13.1 us -> 11.3 us
  starting transfers between devices: 10.3 us -> 8.82 us
  other arithmetic: 0.95 us -> 0 us
    unnamed x26 -> x14, local copies, waits for them, and re-layouts: 8.2 us -> 0.04 us
    pallas_call x1 -> x3, Pallas kernels: 6.64 us -> 3.92 us  [the longest x1 3.86 us: second_pair(): pl.pallas_call(lambda *refs: second_kernel(block, *refs), out_shape=[jax....]
    ppermute x7, waiting for transfers between devices: 9.03 us -> 6.59 us  [swap(): lax.ppermute(value, axis, [(i, i ^ offset) for i in range(lax.axis_size(a...]
    ppermute x7, starting transfers between devices: 10.3 us -> 8.82 us  [swap(): lax.ppermute(value, axis, [(i, i ^ offset) for i in range(lax.axis_size(a...]
    dynamic_update_slice x1 -> x0, other arithmetic: 0.95 us -> none  [gather_group(): out = lax.dynamic_update_index_in_dim(out, block, mine ^ k, 0)]
    pallas_call x1, Pallas kernels: 2.41 us -> 3.18 us  [project(): pl.pallas_call(lambda *refs: project_kernel(rows, window, *refs), out_sha...]
  transfers between devices with their start and end apart: 7 -> 7, of which waited for: 5 -> 4; matrix products, arithmetic and copies ran while one was open for 0% -> 0% of each run, Pallas kernels for 10% -> 15%
where the time goes in v2:
time: 27.7 us; the launch traced here: 27.5 us
  Pallas kernels  11.3 us (41%)
  starting transfers between devices  8.82 us (32%)
  waiting for transfers between devices  6.59 us (24%)
  between operations  0.77 us (3%)
    ppermute x7, starting transfers between devices, swap(): lax.ppermute(value, axis, [(i, i ^ offset) for i in range(lax.axis_size(a...  8.82 us
    ppermute x7, waiting for transfers between devices, swap(): lax.ppermute(value, axis, [(i, i ^ offset) for i in range(lax.axis_size(a...  6.59 us
    pallas_call x1, Pallas kernels, second_pair(): pl.pallas_call(lambda *refs: second_kernel(block, *refs), out_shape=[jax....  3.86 us
    pallas_call x1, Pallas kernels, project(): pl.pallas_call(lambda *refs: project_kernel(rows, window, *refs), out_sha...  3.18 us
    pallas_call x1, Pallas kernels, hermitian(): pl.pallas_call(hermitian_kernel, out_shape=[jax.ShapeDtypeStruct((edge, e...  2.45 us
    pallas_call x1, Pallas kernels, first_pair(): pl.pallas_call(first_kernel, out_shape=jax.ShapeDtypeStruct((edge, 2 * ed...  1.72 us
  transfers between devices with their start and end apart: 7, of which 4 were waited for; matrix products, arithmetic and copies ran while one was open for 0% of the time, Pallas kernels for 15%

profile of v2, /device:TPU:0, one launch (start us, length us, event | category | flops | bytes accessed | tf_op | source)
XLA Modules:
  0.0 27.5 jit_solution(12607853050463757106)
XLA Ops:
  0.6 0.0 copy-start.6
  0.6 3.2 %project.1.refs_0_ = bf16[128,256]{1,0:T(8,128)(2,1)S(1)} custom-call(s32[5]{0:T(128)} %refs_0_.1, s32[4]{0:T(128)} %refs_1_.1, s32[4]{0:T(128)} %refs_2_.1, s32[4]{0:T(128)} %refs_3_.1, bf16[5,8,256,256]{3,2,1,0:T(8,128)(2,1)} %refs_4_.2), custom_call_target="tpu_custom_call" | custom-call | tf_op jit(solution)/shard_map/project/pallas_call | solution.py:134
  3.8 0.0 copy-start
  3.8 0.0 copy-start.1
  3.9 0.0 copy-start.2
  3.9 4.6 %collective-permute-start.2 = (bf16[128,256]{1,0:T(8,128)(2,1)S(1)}, bf16[128,256]{1,0:T(8,128)(2,1)S(1)}, u32[]{:S(2)}, u32[]{:S(2)}) collective-permute-start(bf16[128,256]{1,0:T(8,128)(2,1)S(1)} %project.1.refs_0_), channel_id=1, source_target_pairs={{0,3},{1,2},{2,1},{3,0},{4,7},{5,6},{6,5},{7,4},{8,11},{9,10},{10,... | collective-permute-start | bytes 196616 | tf_op jit(solution)/shard_map/ppermute | solution.py:336
  8.4 0.0 collective-permute-start.1
  8.4 0.6 %collective-permute-start = (bf16[128,256]{1,0:T(8,128)(2,1)S(1)}, bf16[128,256]{1,0:T(8,128)(2,1)S(1)}, u32[]{:S(2)}, u32[]{:S(2)}) collective-permute-start(bf16[128,256]{1,0:T(8,128)(2,1)S(1)} %project.1.refs_0_), channel_id=1, source_target_pairs={{0,1},{1,0},{2,3},{3,2},{4,5},{5,4},{6,7},{7,6},{8,9},{9,8},{10,11... | collective-permute-start | bytes 196616 | tf_op jit(solution)/shard_map/ppermute | solution.py:336
  9.1 0.0 copy-done.6
  9.1 0.0 copy-start.3
  9.1 0.0 copy-start.4
  9.1 0.0 copy-start.5
  9.1 2.4 %hermitian.1 = (f32[512,512]{1,0:T(8,128)S(1)}, f32[512,512]{1,0:T(8,128)S(1)}) custom-call(bf16[512,1024]{1,0:T(8,128)(2,1)S(1)} %bitcast.9), custom_call_target="tpu_custom_call" | custom-call | flops 2147483648 | bytes 3145728 | tf_op jit(solution)/shard_map/hermitian/pallas_call | solution.py:203
  11.5 0.0 collective-permute-done.2.refs_3_
  11.5 2.7 %collective-permute-done.1.refs_2_ = bf16[128,256]{1,0:T(8,128)(2,1)S(1)} collective-permute-done((bf16[128,256]{1,0:T(8,128)(2,1)S(1)}, bf16[128,256]{1,0:T(8,128)(2,1)S(1)}, u32[]{:S(2)}, u32[]{:S(2)}) %collective-permute-start.1) | collective-permute-done | bytes 65568 | tf_op jit(solution)/shard_map/ppermute | solution.py:336
  14.3 0.0 collective-permute-done.refs_1_
  14.3 2.6 %collective-permute-start.5 = (bf16[1,128,256]{2,1,0:T(8,128)(2,1)S(1)}, bf16[1,128,256]{2,1,0:T(8,128)(2,1)S(1)}, u32[]{:S(2)}, u32[]{:S(2)}) collective-permute-start(bf16[1,128,256]{2,1,0:T(8,128)(2,1)S(1)} %bitcast.5), channel_id=1, source_target_pairs={{0,24},{4,28},{8,16},{12,20},{16,8},{20,12},{24,0},{28,4},{1,25},{... | collective-permute-start | bytes 196616 | tf_op jit(solution)/shard_map/ppermute | solution.py:336
  16.9 0.5 %collective-permute-start.4 = (bf16[1,128,256]{2,1,0:T(8,128)(2,1)S(1)}, bf16[1,128,256]{2,1,0:T(8,128)(2,1)S(1)}, u32[]{:S(2)}, u32[]{:S(2)}) collective-permute-start(bf16[1,128,256]{2,1,0:T(8,128)(2,1)S(1)} %bitcast.6), channel_id=1, source_target_pairs={{0,16},{4,20},{8,24},{12,28},{16,0},{20,4},{24,8},{28,12},{1,17},{... | collective-permute-start | bytes 196616 | tf_op jit(solution)/shard_map/ppermute | solution.py:336
  17.5 0.4 %collective-permute-start.3 = (bf16[1,128,256]{2,1,0:T(8,128)(2,1)S(1)}, bf16[1,128,256]{2,1,0:T(8,128)(2,1)S(1)}, u32[]{:S(2)}, u32[]{:S(2)}) collective-permute-start(bf16[1,128,256]{2,1,0:T(8,128)(2,1)S(1)} %bitcast.7), channel_id=1, source_target_pairs={{0,8},{4,12},{8,0},{12,4},{16,24},{20,28},{24,16},{28,20},{1,9},{5... | collective-permute-start | bytes 196616 | tf_op jit(solution)/shard_map/ppermute | solution.py:336
  17.9 2.1 %collective-permute-done.5.refs_3_ = bf16[1,128,256]{2,1,0:T(8,128)(2,1)S(1)} collective-permute-done((bf16[1,128,256]{2,1,0:T(8,128)(2,1)S(1)}, bf16[1,128,256]{2,1,0:T(8,128)(2,1)S(1)}, u32[]{:S(2)}, u32[]{:S(2)}) %collective-permute-start.5) | collective-permute-done | bytes 65568 | tf_op jit(solution)/shard_map/ppermute | solution.py:336
  20.0 1.2 %collective-permute-done.4.refs_2_ = bf16[1,128,256]{2,1,0:T(8,128)(2,1)S(1)} collective-permute-done((bf16[1,128,256]{2,1,0:T(8,128)(2,1)S(1)}, bf16[1,128,256]{2,1,0:T(8,128)(2,1)S(1)}, u32[]{:S(2)}, u32[]{:S(2)}) %collective-permute-start.4) | collective-permute-done | bytes 65568 | tf_op jit(solution)/shard_map/ppermute | solution.py:336
  21.2 0.5 %collective-permute-done.3.refs_1_ = bf16[1,128,256]{2,1,0:T(8,128)(2,1)S(1)} collective-permute-done((bf16[1,128,256]{2,1,0:T(8,128)(2,1)S(1)}, bf16[1,128,256]{2,1,0:T(8,128)(2,1)S(1)}, u32[]{:S(2)}, u32[]{:S(2)}) %collective-permute-start.3) | collective-permute-done | bytes 65568 | tf_op jit(solution)/shard_map/ppermute | solution.py:336
  21.8 0.1 collective-permute-start.6
  21.8 0.0 copy-done
  21.8 0.0 copy-done.1
  21.9 0.0 copy-done.2
  21.9 1.7 %first_pair.1.refs_1_ = bf16[512,1024]{1,0:T(8,128)(2,1)S(1)} custom-call(bf16[4,128,256]{2,1,0:T(8,128)(2,1)S(1)} %bitcast.4, f32[512,512]{1,0:T(8,128)S(1)} %get-tuple-element.17.real_ref.refs_2_, f32[512,512]{1,0:T(8,128)S(1)} %get-tuple-element.18.imag_ref.refs_3_, bf16[512,1024]{1,0:T(8,128)(2,1)S(1)} %copy-done, bf16[4,256,256]{2,1,0:T(8,128)(2,1)S(1)} %copy-done.2, ...), custom_call_target="tpu_custom_call" | custom-call | flops 805306368 | bytes 3145728 | tf_op jit(solution)/shard_map/first_pair/pallas_call | solution.py:260
  23.6 0.0 collective-permute-done.6.refs_0_
  23.6 0.0 copy-done.3
  23.6 0.0 copy-done.4
  23.6 0.0 copy-done.5
  23.6 3.9 %second_pair.1 = (f32[1,512,512]{2,1,0:T(8,128)}, f32[1,512,512]{2,1,0:T(8,128)}, f32[1,512,512]{2,1,0:T(8,128)}) custom-call(bf16[4,128,256]{2,1,0:T(8,128)(2,1)S(1)} %collective-permute-done.6.refs_0_, bf16[512,1024]{1,0:T(8,128)(2,1)S(1)} %first_pair.1.refs_1_, f32[512,512]{1,0:T(8,128)S(1)} %get-tuple-element.17.real_ref.refs_2_, ...), custom_call_target="tpu_custom_call" | custom-call | flops 1342177280 | bytes 10485760 | tf_op jit(solution)/shard_map/second_pair/pallas_call | solution.py:316
  (2 shorter events, 0.1 us)
Async XLA Ops:
  0.6 8.4 %copy-start.6 = (bf16[1,512,1024]{2,1,0:T(8,128)(2,1)S(1)}, bf16[1,512,1024]{2,1,0:T(8,128)(2,1)}, u32[]{:S(2)}) copy-start(bf16[1,512,1024]{2,1,0:T(8,128)(2,1)} %param.17) | copy-start | bytes 3145732
  3.8 18.0 %copy-start = (bf16[512,1024]{1,0:T(8,128)(2,1)S(1)}, bf16[512,1024]{1,0:T(8,128)(2,1)}, u32[]{:S(2)}) copy-start(bf16[512,1024]{1,0:T(8,128)(2,1)} %constant.6.clone.row_ref.refs_4_) | copy-start | bytes 3145732
  3.8 18.0 %copy-start.1 = (bf16[4,256,256]{2,1,0:T(8,128)(2,1)S(1)}, bf16[4,256,256]{2,1,0:T(8,128)(2,1)}, u32[]{:S(2)}) copy-start(bf16[4,256,256]{2,1,0:T(8,128)(2,1)} %constant.8.clone.quadt_ref.refs_6_) | copy-start | bytes 1572868
  3.9 18.0 %copy-start.2 = (bf16[4,256,256]{2,1,0:T(8,128)(2,1)S(1)}, bf16[4,256,256]{2,1,0:T(8,128)(2,1)}, u32[]{:S(2)}) copy-start(bf16[4,256,256]{2,1,0:T(8,128)(2,1)} %constant.7.clone.quad_ref.refs_5_) | copy-start | bytes 1572868
  3.9 7.7 %collective-permute-start.2 = (bf16[128,256]{1,0:T(8,128)(2,1)S(1)}, bf16[128,256]{1,0:T(8,128)(2,1)S(1)}, u32[]{:S(2)}, u32[]{:S(2)}) collective-permute-start(bf16[128,256]{1,0:T(8,128)(2,1)S(1)} %project.1.refs_0_), channel_id=1, source_target_pairs={{0,3},{1,2},{2,1},{3,0},{4,7},{5,6},{6,5},{7,4},{8,11},{9,10},{10,... | collective-permute-start | bytes 196616 | tf_op jit(solution)/shard_map/ppermute | solution.py:336
  8.4 5.9 %collective-permute-start.1 = (bf16[128,256]{1,0:T(8,128)(2,1)S(1)}, bf16[128,256]{1,0:T(8,128)(2,1)S(1)}, u32[]{:S(2)}, u32[]{:S(2)}) collective-permute-start(bf16[128,256]{1,0:T(8,128)(2,1)S(1)} %project.1.refs_0_), channel_id=1, source_target_pairs={{0,2},{1,3},{2,0},{3,1},{4,6},{5,7},{6,4},{7,5},{8,10},{9,11},{10,... | collective-permute-start | bytes 196616 | tf_op jit(solution)/shard_map/ppermute | solution.py:336
  8.4 5.9 %collective-permute-start = (bf16[128,256]{1,0:T(8,128)(2,1)S(1)}, bf16[128,256]{1,0:T(8,128)(2,1)S(1)}, u32[]{:S(2)}, u32[]{:S(2)}) collective-permute-start(bf16[128,256]{1,0:T(8,128)(2,1)S(1)} %project.1.refs_0_), channel_id=1, source_target_pairs={{0,1},{1,0},{2,3},{3,2},{4,5},{5,4},{6,7},{7,6},{8,9},{9,8},{10,11... | collective-permute-start | bytes 196616 | tf_op jit(solution)/shard_map/ppermute | solution.py:336
  9.1 14.5 %copy-start.3 = (f32[1,512,512]{2,1,0:T(8,128)S(1)}, f32[1,512,512]{2,1,0:T(8,128)}, u32[]{:S(2)}) copy-start(f32[1,512,512]{2,1,0:T(8,128)} %refs_7_.1) | copy-start | bytes 3145732
  9.1 14.5 %copy-start.4 = (f32[1,512,512]{2,1,0:T(8,128)S(1)}, f32[1,512,512]{2,1,0:T(8,128)}, u32[]{:S(2)}) copy-start(f32[1,512,512]{2,1,0:T(8,128)} %refs_8_.1) | copy-start | bytes 3145732
  9.1 14.6 %copy-start.5 = (f32[1,512,512]{2,1,0:T(8,128)S(1)}, f32[1,512,512]{2,1,0:T(8,128)}, u32[]{:S(2)}) copy-start(f32[1,512,512]{2,1,0:T(8,128)} %refs_9_.1) | copy-start | bytes 3145732
  14.3 5.7 %collective-permute-start.5 = (bf16[1,128,256]{2,1,0:T(8,128)(2,1)S(1)}, bf16[1,128,256]{2,1,0:T(8,128)(2,1)S(1)}, u32[]{:S(2)}, u32[]{:S(2)}) collective-permute-start(bf16[1,128,256]{2,1,0:T(8,128)(2,1)S(1)} %bitcast.5), channel_id=1, source_target_pairs={{0,24},{4,28},{8,16},{12,20},{16,8},{20,12},{24,0},{28,4},{1,25},{... | collective-permute-start | bytes 196616 | tf_op jit(solution)/shard_map/ppermute | solution.py:336
  16.9 4.3 %collective-permute-start.4 = (bf16[1,128,256]{2,1,0:T(8,128)(2,1)S(1)}, bf16[1,128,256]{2,1,0:T(8,128)(2,1)S(1)}, u32[]{:S(2)}, u32[]{:S(2)}) collective-permute-start(bf16[1,128,256]{2,1,0:T(8,128)(2,1)S(1)} %bitcast.6), channel_id=1, source_target_pairs={{0,16},{4,20},{8,24},{12,28},{16,0},{20,4},{24,8},{28,12},{1,17},{... | collective-permute-start | bytes 196616 | tf_op jit(solution)/shard_map/ppermute | solution.py:336
  17.5 4.3 %collective-permute-start.3 = (bf16[1,128,256]{2,1,0:T(8,128)(2,1)S(1)}, bf16[1,128,256]{2,1,0:T(8,128)(2,1)S(1)}, u32[]{:S(2)}, u32[]{:S(2)}) collective-permute-start(bf16[1,128,256]{2,1,0:T(8,128)(2,1)S(1)} %bitcast.7), channel_id=1, source_target_pairs={{0,8},{4,12},{8,0},{12,4},{16,24},{20,28},{24,16},{28,20},{1,9},{5... | collective-permute-start | bytes 196616 | tf_op jit(solution)/shard_map/ppermute | solution.py:336
  21.8 1.8 %collective-permute-start.6 = (bf16[4,128,256]{2,1,0:T(8,128)(2,1)S(1)}, bf16[4,128,256]{2,1,0:T(8,128)(2,1)S(1)}, u32[]{:S(2)}, u32[]{:S(2)}) collective-permute-start(bf16[4,128,256]{2,1,0:T(8,128)(2,1)S(1)} %bitcast.3), channel_id=1, source_target_pairs={{0,4},{4,0},{8,12},{12,8},{16,20},{20,16},{24,28},{28,24},{1,5},{5... | collective-permute-start | bytes 786440 | tf_op jit(solution)/shard_map/ppermute | solution.py:336

commit v3 on v2

--- a/solution.py
+++ b/solution.py
@@ -69,9 +69,10 @@
 
 def project_kernel(
     rows, window, slot_hbm, orient_hbm, lo_hbm, hi_hbm, map_ref, out_ref,
-    slabs, diff_x, diff_y, sheared, right, acc, sems, slot_ref, orient_ref, lo_ref, hi_ref, param_sems,
+    slabs, diff_y, right, acc, sems, slot_ref, orient_ref, lo_ref, hi_ref, param_sems, *shifted,
 ):
     slots, depth, box = map_ref.shape[0], map_ref.shape[1], map_ref.shape[2]
+    half = box // 2
     me = lax.axis_index("mic")
     orient = (me % 2) * 2 + (me // 2) % 2
     first = (me // 4) * rows
@@ -90,6 +91,16 @@
     for i in range(slots):
         fetch(i).start()
 
+    d = lax.broadcasted_iota(jnp.int32, (box, box), 0)
+    c = lax.broadcasted_iota(jnp.int32, (box, box), 1)
+    diff_y[...] = (d - c).astype(diff_y.dtype)
+    acc[...] = jnp.zeros_like(acc)
+    right[...] = jnp.zeros_like(right)
+    for ref in shifted:
+        ref[...] = jnp.zeros_like(ref)
+    bands = ((slice(0, half + 32), slice(0, half)), (slice(half - 32, box), slice(half, box)))
+    place = pl.ds(pl.multiple_of(base - first + 64, 16), window)
+
     for copy in params:
         copy.wait()
     step = jnp.full((8, 128), orient_ref[orient], jnp.int32).astype(F32)
@@ -98,32 +109,42 @@
     slope_y = jnp.max(radius * jnp.sin(GOLDEN_ANGLE * step))
     low, high = lo_ref[orient], hi_ref[orient]
 
-    a = lax.broadcasted_iota(jnp.int32, (rows, window), 0)
-    b = lax.broadcasted_iota(jnp.int32, (rows, window), 1)
-    diff_x[...] = (b - a + (base - first)).astype(diff_x.dtype)
-    d = lax.broadcasted_iota(jnp.int32, (box, box), 0)
-    c = lax.broadcasted_iota(jnp.int32, (box, box), 1)
-    diff_y[...] = (d - c).astype(diff_y.dtype)
-    acc[...] = jnp.zeros_like(acc)
-    right[...] = jnp.zeros_like(right)
-    half = box // 2
-    bands = ((slice(0, half + 32), slice(0, half)), (slice(half - 32, box), slice(half, box)))
-
     for i in range(slots):
         fetch(i).wait()
         slab = slot_ref[i]
 
         @pl.when((slab >= low) & (slab < high))
         def _():
+            depths = [(slab * depth + j).astype(F32) - (SLABS * SLAB_Z - 1) / 2.0 for j in range(depth)]
+
+            def across(j):
+                for ds, cs in bands:
+                    right[j, ds, cs] = two_taps(diff_y[ds, cs], slope_y * depths[j])
+                moved = dot(slabs[i, j], right[j])
+                shifted[2 * j][place, :] = moved[:, :half]
+                shifted[2 * j + 1][place, :] = moved[:, half:]
+
+            def down(j, total):
+                shift = slope_x * depths[j]
+                whole = jnp.floor(shift)
+                start = whole.astype(jnp.int32) + 64
+                near = jnp.full((1, half), 1.0 - (shift - whole), F32).astype(BF16).astype(F32)
+                far = jnp.full((1, half), shift - whole, F32).astype(BF16).astype(F32)
+                return [
+                    total[n] + near * shifted[2 * j + n][pl.ds(start, rows), :] + far * shifted[2 * j + n][pl.ds(start + 1, rows), :]
+                    for n in range(2)
+                ]
+
+            total = [acc[0], acc[1]]
+            across(0)
             for j in range(depth):
-                z = (slab * depth + j).astype(F32) - (SLABS * SLAB_Z - 1) / 2.0
-                left = two_taps(diff_x[...], slope_x * z)
-                sheared[:, j * box : (j + 1) * box] = dot(left, slabs[i, j]).astype(BF16)
-                for ds, cs in bands:
-                    right[j * box + ds.start : j * box + ds.stop, cs] = two_taps(diff_y[ds, cs], slope_y * z)
-            acc[...] += dot(sheared[...], right[...])
-
-    out_ref[...] = acc[...].astype(BF16)
+                if j + 1 < depth:
+                    across(j + 1)
+                total = down(j, total)
+            acc[0], acc[1] = total
+
+    out_ref[:, :half] = acc[0].astype(BF16)
+    out_ref[:, half:] = acc[1].astype(BF16)
 
 
 def project(map_slabs, slot_slab, orient_index, slab_lo, slab_hi, rows):
@@ -138,18 +159,17 @@
         out_specs=pl.BlockSpec(memory_space=pltpu.VMEM),
         scratch_shapes=[
             pltpu.VMEM((slots, depth, window, box), BF16),
-            pltpu.VMEM((rows, window), TAP),
             pltpu.VMEM((box, box), TAP),
-            pltpu.VMEM((rows, depth * box), BF16),
-            pltpu.VMEM((depth * box, box), BF16),
-            pltpu.VMEM((rows, box), F32),
+            pltpu.VMEM((depth, box, box), BF16),
+            pltpu.VMEM((2, rows, box // 2), F32),
             pltpu.SemaphoreType.DMA((slots,)),
             pltpu.SMEM(slot_slab.shape, jnp.int32),
             pltpu.SMEM(orient_index.shape, jnp.int32),
             pltpu.SMEM(orient_index.shape, jnp.int32),
             pltpu.SMEM(orient_index.shape, jnp.int32),
             pltpu.SemaphoreType.DMA((4,)),
-        ],
+        ]
+        + [pltpu.VMEM((window + 96, box // 2), F32)] * (2 * depth),
         compiler_params=pltpu.CompilerParams(vmem_limit_bytes=16 << 20),
         name="project",
     )(*args)
@@ -219,26 +239,34 @@
     for q in range(count):
         stack[(q // 2) * rows : (q // 2 + 1) * rows, (q % 2) * box : (q % 2 + 1) * box] = pieces_ref[q]
     width = 2 * quarter
+    inputs = {}
     for gh in range(edge // width):
-        cols = slice(gh * width, (gh + 1) * width)
         rr = dot(stack[...], row_ref[:, gh * width : (gh + 1) * width])
         ri = dot(stack[...], row_ref[:, edge + gh * width : edge + (gh + 1) * width])
         r0, r1 = rr[:quarter], rr[quarter:]
         i0, i1 = ri[:quarter], ri[quarter:]
-        inputs = ((r0 + r1, i0 + i1), (r0 + i1, i0 - r1), (r0 - r1, i0 - i1), (r0 - i1, i0 + r1))
-        parts = []
-        for r in range(4):
-            u = jnp.concatenate(inputs[r], axis=0).astype(BF16)
-            spec = dot(quad_ref[r], u)
-            sr, si = spec[:quarter], spec[quarter:]
-            fr = slice(r * quarter, (r + 1) * quarter)
-            tr, ti = real_ref[fr, cols], imag_ref[fr, cols]
-            product = jnp.concatenate([tr * sr + ti * si, ti * sr - tr * si], axis=0).astype(BF16)
-            parts.append(dot(quadt_ref[r], product))
-        ar, ai = parts[0][:quarter] + parts[2][:quarter], parts[0][quarter:] + parts[2][quarter:]
-        br, bi = parts[0][:quarter] - parts[2][:quarter], parts[0][quarter:] - parts[2][quarter:]
-        cr, ci = parts[1][:quarter] + parts[3][:quarter], parts[1][quarter:] + parts[3][quarter:]
-        dr, di = parts[1][:quarter] - parts[3][:quarter], parts[1][quarter:] - parts[3][quarter:]
+        for r, pair in enumerate(((r0 + r1, i0 + i1), (r0 + i1, i0 - r1), (r0 - r1, i0 - i1), (r0 - i1, i0 + r1))):
+            inputs[gh, r] = jnp.concatenate(pair, axis=0).astype(BF16)
+    items = [(gh, r) for gh in range(edge // width) for r in range(4)]
+    parts = {}
+
+    def spectrum(gh, r):
+        return dot(quad_ref[r], inputs[gh, r])
+
+    def back(gh, r, spec):
+        cols = slice(gh * width, (gh + 1) * width)
+        sr, si = spec[:quarter], spec[quarter:]
+        fr = slice(r * quarter, (r + 1) * quarter)
+        tr, ti = real_ref[fr, cols], imag_ref[fr, cols]
+        product = jnp.concatenate([tr * sr + ti * si, ti * sr - tr * si], axis=0).astype(BF16)
+        parts[gh, r] = dot(quadt_ref[r], product)
+
+    def combine(gh):
+        part = [parts[gh, r] for r in range(4)]
+        ar, ai = part[0][:quarter] + part[2][:quarter], part[0][quarter:] + part[2][quarter:]
+        br, bi = part[0][:quarter] - part[2][:quarter], part[0][quarter:] - part[2][quarter:]
+        cr, ci = part[1][:quarter] + part[3][:quarter], part[1][quarter:] + part[3][quarter:]
+        dr, di = part[1][:quarter] - part[3][:quarter], part[1][quarter:] - part[3][quarter:]
         outs = ((ar + cr, ai + ci), (br - di, bi + dr), (ar - cr, ai - ci), (br + di, bi - dr))
         for k in range(4):
             xs = slice(k * quarter, (k + 1) * quarter)
@@ -248,6 +276,16 @@
                 start = (2 * gh + t) * width
                 half[xs, start : start + quarter] = hr[:, lanes]
                 half[xs, start + quarter : start + width] = hi[:, lanes]
+
+    ahead = 1
+    specs = {item: spectrum(*item) for item in items[:ahead]}
+    for n, item in enumerate(items):
+        if n + ahead < len(items):
+            specs[items[n + ahead]] = spectrum(*items[n + ahead])
+        back(*item, specs.pop(item))
+        if n % 4 == 1 and n > 4:
+            combine(n // 4 - 1)
+    combine(len(items) // 4 - 1)
 
 
 def first_kernel(pieces_ref, real_ref, imag_ref, row_ref, quad_ref, quadt_ref, half_ref, stack):
@@ -269,9 +307,12 @@
     )(pieces, th_real, th_imag, row, quad, quad_t)
 
 
-def scores_of(half, quad_ref, quarter):
+def columns_of(half, quad_ref, quarter):
     width = 2 * quarter
-    f = [dot(half[:, s * width : (s + 1) * width], quad_ref[s]) for s in range(4)]
+    return [dot(half[:, s * width : (s + 1) * width], quad_ref[s]) for s in range(4)]
+
+
+def scores_of(f, quarter):
     re = [x[:, :quarter] for x in f]
     im = [x[:, quarter:] for x in f]
     ar, ai, br, bi = re[0] + re[2], im[0] + im[2], re[0] - re[2], im[0] - im[2]
@@ -287,10 +328,18 @@
     quarter = edge // 4
     half_transform(pieces_ref, real_ref, imag_ref, row_ref, quad_ref, quadt_ref, stack, other)
     copies = []
-    for step in range(edge // block):
+    steps = edge // block
+
+    def columns(step):
         xs = slice(step * block, (step + 1) * block)
-        one = scores_of(half_ref[xs, :], quad_ref, quarter)
-        two = scores_of(other[xs, :], quad_ref, quarter)
+        return columns_of(half_ref[xs, :], quad_ref, quarter), columns_of(other[xs, :], quad_ref, quarter)
+
+    ready = columns(0)
+    for step in range(steps):
+        xs = slice(step * block, (step + 1) * block)
+        one, two = (scores_of(x, quarter) for x in ready)
+        if step + 1 < steps:
+            ready = columns(step + 1)
         for k in range(4):
             ys = slice(k * quarter, (k + 1) * quarter)
             best, total, square = max_ref[0, xs, ys], sum_ref[0, xs, ys], sq_ref[0, xs, ys]

time: 27.7 us -> 27.2 us (0.982)
  Pallas kernels: 11.3 us -> 9.5 us
  starting transfers between devices: 8.82 us -> 9.38 us
  waiting for transfers between devices: 6.59 us -> 7.07 us
    pallas_call x1, Pallas kernels: 3.18 us -> 2.08 us  [project(): pl.pallas_call(lambda *refs: project_kernel(rows, window, *refs), out_sha...]
    ppermute x7, starting transfers between devices: 8.82 us -> 9.38 us  [swap(): lax.ppermute(value, axis, [(i, i ^ offset) for i in range(lax.axis_size(a...]
    ppermute x7, waiting for transfers between devices: 6.59 us -> 7.07 us  [swap(): lax.ppermute(value, axis, [(i, i ^ offset) for i in range(lax.axis_size(a...]
    pallas_call x1, Pallas kernels: 1.72 us -> 1.37 us  [first_pair(): pl.pallas_call(first_kernel, out_shape=jax.ShapeDtypeStruct((edge, 2 * ed...]
    pallas_call x1, Pallas kernels: 3.86 us -> 3.53 us  [second_pair(): pl.pallas_call(lambda *refs: second_kernel(block, *refs), out_shape=[jax....]
  transfers between devices with their start and end apart: 7 -> 7, of which waited for: 4 -> 5; matrix products, arithmetic and copies ran while one was open for 0% -> 0% of each run, Pallas kernels for 15% -> 14%
where the time goes in v3:
time: 27.2 us; the launch traced here: 26.7 us
  Pallas kernels  9.5 us (35%)
  starting transfers between devices  9.38 us (34%)
  waiting for transfers between devices  7.07 us (26%)
  between operations  0.75 us (3%)
    ppermute x7, starting transfers between devices, swap(): lax.ppermute(value, axis, [(i, i ^ offset) for i in range(lax.axis_size(a...  9.38 us
    ppermute x7, waiting for transfers between devices, swap(): lax.ppermute(value, axis, [(i, i ^ offset) for i in range(lax.axis_size(a...  7.07 us
    pallas_call x1, Pallas kernels, second_pair(): pl.pallas_call(lambda *refs: second_kernel(block, *refs), out_shape=[jax....  3.53 us
    pallas_call x1, Pallas kernels, hermitian(): pl.pallas_call(hermitian_kernel, out_shape=[jax.ShapeDtypeStruct((edge, e...  2.45 us
    pallas_call x1, Pallas kernels, project(): pl.pallas_call(lambda *refs: project_kernel(rows, window, *refs), out_sha...  2.08 us
    pallas_call x1, Pallas kernels, first_pair(): pl.pallas_call(first_kernel, out_shape=jax.ShapeDtypeStruct((edge, 2 * ed...  1.37 us
  transfers between devices with their start and end apart: 7, of which 5 were waited for; matrix products, arithmetic and copies ran while one was open for 0% of the time, Pallas kernels for 14%

profile of v3, /device:TPU:0, one launch (start us, length us, event | category | flops | bytes accessed | tf_op | source)
XLA Modules:
  0.0 26.7 jit_solution(9465340152238346670)
XLA Ops:
  0.6 0.0 copy-start.6
  0.6 2.1 %project.1.refs_0_ = bf16[128,256]{1,0:T(8,128)(2,1)S(1)} custom-call(s32[5]{0:T(128)} %refs_0_.1, s32[4]{0:T(128)} %refs_1_.1, s32[4]{0:T(128)} %refs_2_.1, s32[4]{0:T(128)} %refs_3_.1, bf16[5,8,256,256]{3,2,1,0:T(8,128)(2,1)} %refs_4_.2), custom_call_target="tpu_custom_call" | custom-call | tf_op jit(solution)/shard_map/project/pallas_call | solution.py:155
  2.7 0.0 copy-start
  2.7 0.0 copy-start.1
  2.8 0.0 copy-start.2
  2.8 5.1 %collective-permute-start.2 = (bf16[128,256]{1,0:T(8,128)(2,1)S(1)}, bf16[128,256]{1,0:T(8,128)(2,1)S(1)}, u32[]{:S(2)}, u32[]{:S(2)}) collective-permute-start(bf16[128,256]{1,0:T(8,128)(2,1)S(1)} %project.1.refs_0_), channel_id=1, source_target_pairs={{0,3},{1,2},{2,1},{3,0},{4,7},{5,6},{6,5},{7,4},{8,11},{9,10},{10,... | collective-permute-start | bytes 196616 | tf_op jit(solution)/shard_map/ppermute | solution.py:385
  7.9 0.0 collective-permute-start.1
  7.9 0.6 %collective-permute-start = (bf16[128,256]{1,0:T(8,128)(2,1)S(1)}, bf16[128,256]{1,0:T(8,128)(2,1)S(1)}, u32[]{:S(2)}, u32[]{:S(2)}) collective-permute-start(bf16[128,256]{1,0:T(8,128)(2,1)S(1)} %project.1.refs_0_), channel_id=1, source_target_pairs={{0,1},{1,0},{2,3},{3,2},{4,5},{5,4},{6,7},{7,6},{8,9},{9,8},{10,11... | collective-permute-start | bytes 196616 | tf_op jit(solution)/shard_map/ppermute | solution.py:385
  8.5 0.0 copy-done.6
  8.5 0.0 copy-start.3
  8.5 0.0 copy-start.4
  8.5 0.0 copy-start.5
  8.5 2.4 %hermitian.1 = (f32[512,512]{1,0:T(8,128)S(1)}, f32[512,512]{1,0:T(8,128)S(1)}) custom-call(bf16[512,1024]{1,0:T(8,128)(2,1)S(1)} %bitcast.9), custom_call_target="tpu_custom_call" | custom-call | flops 2147483648 | bytes 3145728 | tf_op jit(solution)/shard_map/hermitian/pallas_call | solution.py:223
  11.0 0.0 collective-permute-done.2.refs_3_
  11.0 3.2 %collective-permute-done.1.refs_2_ = bf16[128,256]{1,0:T(8,128)(2,1)S(1)} collective-permute-done((bf16[128,256]{1,0:T(8,128)(2,1)S(1)}, bf16[128,256]{1,0:T(8,128)(2,1)S(1)}, u32[]{:S(2)}, u32[]{:S(2)}) %collective-permute-start.1) | collective-permute-done | bytes 65568 | tf_op jit(solution)/shard_map/ppermute | solution.py:385
  14.2 0.0 collective-permute-done.refs_1_
  14.2 2.6 %collective-permute-start.5 = (bf16[1,128,256]{2,1,0:T(8,128)(2,1)S(1)}, bf16[1,128,256]{2,1,0:T(8,128)(2,1)S(1)}, u32[]{:S(2)}, u32[]{:S(2)}) collective-permute-start(bf16[1,128,256]{2,1,0:T(8,128)(2,1)S(1)} %bitcast.5), channel_id=1, source_target_pairs={{0,24},{4,28},{8,16},{12,20},{16,8},{20,12},{24,0},{28,4},{1,25},{... | collective-permute-start | bytes 196616 | tf_op jit(solution)/shard_map/ppermute | solution.py:385
  16.8 0.5 %collective-permute-start.4 = (bf16[1,128,256]{2,1,0:T(8,128)(2,1)S(1)}, bf16[1,128,256]{2,1,0:T(8,128)(2,1)S(1)}, u32[]{:S(2)}, u32[]{:S(2)}) collective-permute-start(bf16[1,128,256]{2,1,0:T(8,128)(2,1)S(1)} %bitcast.6), channel_id=1, source_target_pairs={{0,16},{4,20},{8,24},{12,28},{16,0},{20,4},{24,8},{28,12},{1,17},{... | collective-permute-start | bytes 196616 | tf_op jit(solution)/shard_map/ppermute | solution.py:385
  17.3 0.5 %collective-permute-start.3 = (bf16[1,128,256]{2,1,0:T(8,128)(2,1)S(1)}, bf16[1,128,256]{2,1,0:T(8,128)(2,1)S(1)}, u32[]{:S(2)}, u32[]{:S(2)}) collective-permute-start(bf16[1,128,256]{2,1,0:T(8,128)(2,1)S(1)} %bitcast.7), channel_id=1, source_target_pairs={{0,8},{4,12},{8,0},{12,4},{16,24},{20,28},{24,16},{28,20},{1,9},{5... | collective-permute-start | bytes 196616 | tf_op jit(solution)/shard_map/ppermute | solution.py:385
  17.8 1.8 %collective-permute-done.5.refs_3_ = bf16[1,128,256]{2,1,0:T(8,128)(2,1)S(1)} collective-permute-done((bf16[1,128,256]{2,1,0:T(8,128)(2,1)S(1)}, bf16[1,128,256]{2,1,0:T(8,128)(2,1)S(1)}, u32[]{:S(2)}, u32[]{:S(2)}) %collective-permute-start.5) | collective-permute-done | bytes 65568 | tf_op jit(solution)/shard_map/ppermute | solution.py:385
  19.6 1.5 %collective-permute-done.4.refs_2_ = bf16[1,128,256]{2,1,0:T(8,128)(2,1)S(1)} collective-permute-done((bf16[1,128,256]{2,1,0:T(8,128)(2,1)S(1)}, bf16[1,128,256]{2,1,0:T(8,128)(2,1)S(1)}, u32[]{:S(2)}, u32[]{:S(2)}) %collective-permute-start.4) | collective-permute-done | bytes 65568 | tf_op jit(solution)/shard_map/ppermute | solution.py:385
  21.0 0.5 %collective-permute-done.3.refs_1_ = bf16[1,128,256]{2,1,0:T(8,128)(2,1)S(1)} collective-permute-done((bf16[1,128,256]{2,1,0:T(8,128)(2,1)S(1)}, bf16[1,128,256]{2,1,0:T(8,128)(2,1)S(1)}, u32[]{:S(2)}, u32[]{:S(2)}) %collective-permute-start.3) | collective-permute-done | bytes 65568 | tf_op jit(solution)/shard_map/ppermute | solution.py:385
  21.6 0.1 collective-permute-start.6
  21.7 0.0 copy-done
  21.7 0.0 copy-done.1
  21.7 0.0 copy-done.2
  21.7 1.4 %first_pair.1.refs_1_ = bf16[512,1024]{1,0:T(8,128)(2,1)S(1)} custom-call(bf16[4,128,256]{2,1,0:T(8,128)(2,1)S(1)} %bitcast.4, f32[512,512]{1,0:T(8,128)S(1)} %get-tuple-element.17.real_ref.refs_2_, f32[512,512]{1,0:T(8,128)S(1)} %get-tuple-element.18.imag_ref.refs_3_, bf16[512,1024]{1,0:T(8,128)(2,1)S(1)} %copy-done, bf16[4,256,256]{2,1,0:T(8,128)(2,1)S(1)} %copy-done.2, ...), custom_call_target="tpu_custom_call" | custom-call | flops 805306368 | bytes 3145728 | tf_op jit(solution)/shard_map/first_pair/pallas_call | solution.py:298
  23.1 0.1 collective-permute-done.6.refs_0_
  23.2 0.0 copy-done.3
  23.2 0.0 copy-done.4
  23.2 0.0 copy-done.5
  23.2 3.5 %second_pair.1 = (f32[1,512,512]{2,1,0:T(8,128)}, f32[1,512,512]{2,1,0:T(8,128)}, f32[1,512,512]{2,1,0:T(8,128)}) custom-call(bf16[4,128,256]{2,1,0:T(8,128)(2,1)S(1)} %collective-permute-done.6.refs_0_, bf16[512,1024]{1,0:T(8,128)(2,1)S(1)} %first_pair.1.refs_1_, f32[512,512]{1,0:T(8,128)S(1)} %get-tuple-element.17.real_ref.refs_2_, ...), custom_call_target="tpu_custom_call" | custom-call | flops 1342177280 | bytes 10485760 | tf_op jit(solution)/shard_map/second_pair/pallas_call | solution.py:365
  (2 shorter events, 0.1 us)
Async XLA Ops:
  0.6 7.9 %copy-start.6 = (bf16[1,512,1024]{2,1,0:T(8,128)(2,1)S(1)}, bf16[1,512,1024]{2,1,0:T(8,128)(2,1)}, u32[]{:S(2)}) copy-start(bf16[1,512,1024]{2,1,0:T(8,128)(2,1)} %param.17) | copy-start | bytes 3145732
  2.7 18.9 %copy-start = (bf16[512,1024]{1,0:T(8,128)(2,1)S(1)}, bf16[512,1024]{1,0:T(8,128)(2,1)}, u32[]{:S(2)}) copy-start(bf16[512,1024]{1,0:T(8,128)(2,1)} %constant.6.clone.row_ref.refs_4_) | copy-start | bytes 3145732
  2.7 18.9 %copy-start.1 = (bf16[4,256,256]{2,1,0:T(8,128)(2,1)S(1)}, bf16[4,256,256]{2,1,0:T(8,128)(2,1)}, u32[]{:S(2)}) copy-start(bf16[4,256,256]{2,1,0:T(8,128)(2,1)} %constant.8.clone.quadt_ref.refs_6_) | copy-start | bytes 1572868
  2.8 18.9 %copy-start.2 = (bf16[4,256,256]{2,1,0:T(8,128)(2,1)S(1)}, bf16[4,256,256]{2,1,0:T(8,128)(2,1)}, u32[]{:S(2)}) copy-start(bf16[4,256,256]{2,1,0:T(8,128)(2,1)} %constant.7.clone.quad_ref.refs_5_) | copy-start | bytes 1572868
  2.8 8.2 %collective-permute-start.2 = (bf16[128,256]{1,0:T(8,128)(2,1)S(1)}, bf16[128,256]{1,0:T(8,128)(2,1)S(1)}, u32[]{:S(2)}, u32[]{:S(2)}) collective-permute-start(bf16[128,256]{1,0:T(8,128)(2,1)S(1)} %project.1.refs_0_), channel_id=1, source_target_pairs={{0,3},{1,2},{2,1},{3,0},{4,7},{5,6},{6,5},{7,4},{8,11},{9,10},{10,... | collective-permute-start | bytes 196616 | tf_op jit(solution)/shard_map/ppermute | solution.py:385
  7.9 6.3 %collective-permute-start.1 = (bf16[128,256]{1,0:T(8,128)(2,1)S(1)}, bf16[128,256]{1,0:T(8,128)(2,1)S(1)}, u32[]{:S(2)}, u32[]{:S(2)}) collective-permute-start(bf16[128,256]{1,0:T(8,128)(2,1)S(1)} %project.1.refs_0_), channel_id=1, source_target_pairs={{0,2},{1,3},{2,0},{3,1},{4,6},{5,7},{6,4},{7,5},{8,10},{9,11},{10,... | collective-permute-start | bytes 196616 | tf_op jit(solution)/shard_map/ppermute | solution.py:385
  7.9 6.3 %collective-permute-start = (bf16[128,256]{1,0:T(8,128)(2,1)S(1)}, bf16[128,256]{1,0:T(8,128)(2,1)S(1)}, u32[]{:S(2)}, u32[]{:S(2)}) collective-permute-start(bf16[128,256]{1,0:T(8,128)(2,1)S(1)} %project.1.refs_0_), channel_id=1, source_target_pairs={{0,1},{1,0},{2,3},{3,2},{4,5},{5,4},{6,7},{7,6},{8,9},{9,8},{10,11... | collective-permute-start | bytes 196616 | tf_op jit(solution)/shard_map/ppermute | solution.py:385
  8.5 14.7 %copy-start.3 = (f32[1,512,512]{2,1,0:T(8,128)S(1)}, f32[1,512,512]{2,1,0:T(8,128)}, u32[]{:S(2)}) copy-start(f32[1,512,512]{2,1,0:T(8,128)} %refs_7_.1) | copy-start | bytes 3145732
  8.5 14.7 %copy-start.4 = (f32[1,512,512]{2,1,0:T(8,128)S(1)}, f32[1,512,512]{2,1,0:T(8,128)}, u32[]{:S(2)}) copy-start(f32[1,512,512]{2,1,0:T(8,128)} %refs_8_.1) | copy-start | bytes 3145732
  8.5 14.7 %copy-start.5 = (f32[1,512,512]{2,1,0:T(8,128)S(1)}, f32[1,512,512]{2,1,0:T(8,128)}, u32[]{:S(2)}) copy-start(f32[1,512,512]{2,1,0:T(8,128)} %refs_9_.1) | copy-start | bytes 3145732
  14.2 5.3 %collective-permute-start.5 = (bf16[1,128,256]{2,1,0:T(8,128)(2,1)S(1)}, bf16[1,128,256]{2,1,0:T(8,128)(2,1)S(1)}, u32[]{:S(2)}, u32[]{:S(2)}) collective-permute-start(bf16[1,128,256]{2,1,0:T(8,128)(2,1)S(1)} %bitcast.5), channel_id=1, source_target_pairs={{0,24},{4,28},{8,16},{12,20},{16,8},{20,12},{24,0},{28,4},{1,25},{... | collective-permute-start | bytes 196616 | tf_op jit(solution)/shard_map/ppermute | solution.py:385
  16.8 4.3 %collective-permute-start.4 = (bf16[1,128,256]{2,1,0:T(8,128)(2,1)S(1)}, bf16[1,128,256]{2,1,0:T(8,128)(2,1)S(1)}, u32[]{:S(2)}, u32[]{:S(2)}) collective-permute-start(bf16[1,128,256]{2,1,0:T(8,128)(2,1)S(1)} %bitcast.6), channel_id=1, source_target_pairs={{0,16},{4,20},{8,24},{12,28},{16,0},{20,4},{24,8},{28,12},{1,17},{... | collective-permute-start | bytes 196616 | tf_op jit(solution)/shard_map/ppermute | solution.py:385
  17.3 4.3 %collective-permute-start.3 = (bf16[1,128,256]{2,1,0:T(8,128)(2,1)S(1)}, bf16[1,128,256]{2,1,0:T(8,128)(2,1)S(1)}, u32[]{:S(2)}, u32[]{:S(2)}) collective-permute-start(bf16[1,128,256]{2,1,0:T(8,128)(2,1)S(1)} %bitcast.7), channel_id=1, source_target_pairs={{0,8},{4,12},{8,0},{12,4},{16,24},{20,28},{24,16},{28,20},{1,9},{5... | collective-permute-start | bytes 196616 | tf_op jit(solution)/shard_map/ppermute | solution.py:385
  21.6 1.6 %collective-permute-start.6 = (bf16[4,128,256]{2,1,0:T(8,128)(2,1)S(1)}, bf16[4,128,256]{2,1,0:T(8,128)(2,1)S(1)}, u32[]{:S(2)}, u32[]{:S(2)}) collective-permute-start(bf16[4,128,256]{2,1,0:T(8,128)(2,1)S(1)} %bitcast.3), channel_id=1, source_target_pairs={{0,4},{4,0},{8,12},{12,8},{16,20},{20,16},{24,28},{28,24},{1,5},{5... | collective-permute-start | bytes 786440 | tf_op jit(solution)/shard_map/ppermute | solution.py:385

commit v4 on v3

--- a/solution.py
+++ b/solution.py
@@ -240,13 +240,19 @@
         stack[(q // 2) * rows : (q // 2 + 1) * rows, (q % 2) * box : (q % 2 + 1) * box] = pieces_ref[q]
     width = 2 * quarter
     inputs = {}
-    for gh in range(edge // width):
-        rr = dot(stack[...], row_ref[:, gh * width : (gh + 1) * width])
-        ri = dot(stack[...], row_ref[:, edge + gh * width : edge + (gh + 1) * width])
+    rows_of = {}
+
+    def row(gh, part):
+        start = part * edge + gh * width
+        rows_of[gh, part] = dot(stack[...], row_ref[:, start : start + width])
+
+    def fold(gh):
+        rr, ri = rows_of[gh, 0], rows_of[gh, 1]
         r0, r1 = rr[:quarter], rr[quarter:]
         i0, i1 = ri[:quarter], ri[quarter:]
         for r, pair in enumerate(((r0 + r1, i0 + i1), (r0 + i1, i0 - r1), (r0 - r1, i0 - i1), (r0 - i1, i0 + r1))):
             inputs[gh, r] = jnp.concatenate(pair, axis=0).astype(BF16)
+
     items = [(gh, r) for gh in range(edge // width) for r in range(4)]
     parts = {}
 
@@ -277,15 +283,19 @@
                 half[xs, start : start + quarter] = hr[:, lanes]
                 half[xs, start + quarter : start + width] = hi[:, lanes]
 
-    ahead = 1
-    specs = {item: spectrum(*item) for item in items[:ahead]}
-    for n, item in enumerate(items):
-        if n + ahead < len(items):
-            specs[items[n + ahead]] = spectrum(*items[n + ahead])
-        back(*item, specs.pop(item))
-        if n % 4 == 1 and n > 4:
-            combine(n // 4 - 1)
-    combine(len(items) // 4 - 1)
+    specs = {}
+    for token in "R0 R1 R2 R3 U0 S0 S1 S2 S3 U1 S4 B0 S5 B1 S6 B2 S7 B3 B4 B5 C0 B6 B7 C1".split():
+        act, n = token[0], int(token[1])
+        if act == "R":
+            row(n // 2, n % 2)
+        elif act == "U":
+            fold(n)
+        elif act == "S":
+            specs[n] = spectrum(*items[n])
+        elif act == "B":
+            back(*items[n], specs.pop(n))
+        else:
+            combine(n)
 
 
 def first_kernel(pieces_ref, real_ref, imag_ref, row_ref, quad_ref, quadt_ref, half_ref, stack):
@@ -413,7 +423,7 @@
     row, quad, quad_t = constants(box, edge)
 
     part = project(map_slabs, slot_slab, orient_index, slab_lo, slab_hi, rows)
-    got = [swap(part, "proj", k) for k in range(1, lax.axis_size("proj"))]
+    got = [swap(part, "proj", k) for k in sorted(range(1, lax.axis_size("proj")), key=lambda k: (k & (k - 1) == 0 and k > 1, k))]
     tile, _ = lax.optimization_barrier((tile_spectrum[0], part))
     th_real, th_imag = hermitian(tile)
     got, th_real, th_imag = lax.optimization_barrier((got, th_real, th_imag))

time: 27.2 us -> 26.7 us (0.982); the launches traced: 26.7 us -> 26.7 us
  starting transfers between devices: 9.38 us -> 10.7 us
  waiting for transfers between devices: 7.07 us -> 5.92 us
    ppermute x7, starting transfers between devices: 9.38 us -> 10.7 us  [swap(): lax.ppermute(value, axis, [(i, i ^ offset) for i in range(lax.axis_size(a...]
    ppermute x7, waiting for transfers between devices: 7.07 us -> 5.92 us  [swap(): lax.ppermute(value, axis, [(i, i ^ offset) for i in range(lax.axis_size(a...]
  transfers between devices with their start and end apart: 7 -> 7, of which waited for: 5 -> 6; matrix products, arithmetic and copies ran while one was open for 0% -> 0% of each run, Pallas kernels for 14% -> 14%
where the time goes in v4:
time: 26.7 us
  starting transfers between devices  10.7 us (40%)
  Pallas kernels  9.28 us (35%)
  waiting for transfers between devices  5.92 us (22%)
  between operations  0.76 us (3%)
    ppermute x7, starting transfers between devices, swap(): lax.ppermute(value, axis, [(i, i ^ offset) for i in range(lax.axis_size(a...  10.7 us
    ppermute x7, waiting for transfers between devices, swap(): lax.ppermute(value, axis, [(i, i ^ offset) for i in range(lax.axis_size(a...  5.92 us
    pallas_call x1, Pallas kernels, second_pair(): pl.pallas_call(lambda *refs: second_kernel(block, *refs), out_shape=[jax....  3.45 us
    pallas_call x1, Pallas kernels, hermitian(): pl.pallas_call(hermitian_kernel, out_shape=[jax.ShapeDtypeStruct((edge, e...  2.44 us
    pallas_call x1, Pallas kernels, project(): pl.pallas_call(lambda *refs: project_kernel(rows, window, *refs), out_sha...  2.08 us
    pallas_call x1, Pallas kernels, first_pair(): pl.pallas_call(first_kernel, out_shape=jax.ShapeDtypeStruct((edge, 2 * ed...  1.24 us
  transfers between devices with their start and end apart: 7, of which 6 were waited for; matrix products, arithmetic and copies ran while one was open for 0% of the time, Pallas kernels for 14%

profile of v4, /device:TPU:0, one launch (start us, length us, event | category | flops | bytes accessed | tf_op | source)
XLA Modules:
  0.0 26.7 jit_solution(1995775213955387672)
XLA Ops:
  0.6 0.0 copy-start.6
  0.6 2.1 %project.1.refs_0_ = bf16[128,256]{1,0:T(8,128)(2,1)S(1)} custom-call(s32[5]{0:T(128)} %refs_0_.1, s32[4]{0:T(128)} %refs_1_.1, s32[4]{0:T(128)} %refs_2_.1, s32[4]{0:T(128)} %refs_3_.1, bf16[5,8,256,256]{3,2,1,0:T(8,128)(2,1)} %refs_4_.2), custom_call_target="tpu_custom_call" | custom-call | tf_op jit(solution)/shard_map/project/pallas_call | solution.py:155
  2.7 0.0 copy-start
  2.7 0.0 copy-start.1
  2.8 0.0 copy-start.2
  2.8 4.9 %collective-permute-start.2 = (bf16[128,256]{1,0:T(8,128)(2,1)S(1)}, bf16[128,256]{1,0:T(8,128)(2,1)S(1)}, u32[]{:S(2)}, u32[]{:S(2)}) collective-permute-start(bf16[128,256]{1,0:T(8,128)(2,1)S(1)} %project.1.refs_0_), channel_id=1, source_target_pairs={{0,2},{1,3},{2,0},{3,1},{4,6},{5,7},{6,4},{7,5},{8,10},{9,11},{10,... | collective-permute-start | bytes 196616 | tf_op jit(solution)/shard_map/ppermute | solution.py:395
  7.6 2.2 %collective-permute-start.1 = (bf16[128,256]{1,0:T(8,128)(2,1)S(1)}, bf16[128,256]{1,0:T(8,128)(2,1)S(1)}, u32[]{:S(2)}, u32[]{:S(2)}) collective-permute-start(bf16[128,256]{1,0:T(8,128)(2,1)S(1)} %project.1.refs_0_), channel_id=1, source_target_pairs={{0,3},{1,2},{2,1},{3,0},{4,7},{5,6},{6,5},{7,4},{8,11},{9,10},{10,... | collective-permute-start | bytes 196616 | tf_op jit(solution)/shard_map/ppermute | solution.py:395
  9.8 0.0 collective-permute-start
  9.8 0.0 copy-done.6
  9.8 0.0 copy-start.3
  9.8 0.0 copy-start.4
  9.9 0.0 copy-start.5
  9.9 2.4 %hermitian.1 = (f32[512,512]{1,0:T(8,128)S(1)}, f32[512,512]{1,0:T(8,128)S(1)}) custom-call(bf16[512,1024]{1,0:T(8,128)(2,1)S(1)} %bitcast.9), custom_call_target="tpu_custom_call" | custom-call | flops 2147483648 | bytes 3145728 | tf_op jit(solution)/shard_map/hermitian/pallas_call | solution.py:223
  12.3 0.0 collective-permute-done.2.refs_3_
  12.3 1.8 %collective-permute-done.1.refs_2_ = bf16[128,256]{1,0:T(8,128)(2,1)S(1)} collective-permute-done((bf16[128,256]{1,0:T(8,128)(2,1)S(1)}, bf16[128,256]{1,0:T(8,128)(2,1)S(1)}, u32[]{:S(2)}, u32[]{:S(2)}) %collective-permute-start.1) | collective-permute-done | bytes 65568 | tf_op jit(solution)/shard_map/ppermute | solution.py:395
  14.1 0.5 %collective-permute-done.refs_1_ = bf16[128,256]{1,0:T(8,128)(2,1)S(1)} collective-permute-done((bf16[128,256]{1,0:T(8,128)(2,1)S(1)}, bf16[128,256]{1,0:T(8,128)(2,1)S(1)}, u32[]{:S(2)}, u32[]{:S(2)}) %collective-permute-start) | collective-permute-done | bytes 65568 | tf_op jit(solution)/shard_map/ppermute | solution.py:395
  14.7 2.1 %collective-permute-start.5 = (bf16[1,128,256]{2,1,0:T(8,128)(2,1)S(1)}, bf16[1,128,256]{2,1,0:T(8,128)(2,1)S(1)}, u32[]{:S(2)}, u32[]{:S(2)}) collective-permute-start(bf16[1,128,256]{2,1,0:T(8,128)(2,1)S(1)} %bitcast.5), channel_id=1, source_target_pairs={{0,24},{4,28},{8,16},{12,20},{16,8},{20,12},{24,0},{28,4},{1,25},{... | collective-permute-start | bytes 196616 | tf_op jit(solution)/shard_map/ppermute | solution.py:395
  16.8 0.5 %collective-permute-start.4 = (bf16[1,128,256]{2,1,0:T(8,128)(2,1)S(1)}, bf16[1,128,256]{2,1,0:T(8,128)(2,1)S(1)}, u32[]{:S(2)}, u32[]{:S(2)}) collective-permute-start(bf16[1,128,256]{2,1,0:T(8,128)(2,1)S(1)} %bitcast.6), channel_id=1, source_target_pairs={{0,16},{4,20},{8,24},{12,28},{16,0},{20,4},{24,8},{28,12},{1,17},{... | collective-permute-start | bytes 196616 | tf_op jit(solution)/shard_map/ppermute | solution.py:395
  17.3 0.9 %collective-permute-start.3 = (bf16[1,128,256]{2,1,0:T(8,128)(2,1)S(1)}, bf16[1,128,256]{2,1,0:T(8,128)(2,1)S(1)}, u32[]{:S(2)}, u32[]{:S(2)}) collective-permute-start(bf16[1,128,256]{2,1,0:T(8,128)(2,1)S(1)} %bitcast.7), channel_id=1, source_target_pairs={{0,8},{4,12},{8,0},{12,4},{16,24},{20,28},{24,16},{28,20},{1,9},{5... | collective-permute-start | bytes 196616 | tf_op jit(solution)/shard_map/ppermute | solution.py:395
  18.2 1.7 %collective-permute-done.5.refs_3_ = bf16[1,128,256]{2,1,0:T(8,128)(2,1)S(1)} collective-permute-done((bf16[1,128,256]{2,1,0:T(8,128)(2,1)S(1)}, bf16[1,128,256]{2,1,0:T(8,128)(2,1)S(1)}, u32[]{:S(2)}, u32[]{:S(2)}) %collective-permute-start.5) | collective-permute-done | bytes 65568 | tf_op jit(solution)/shard_map/ppermute | solution.py:395
  19.9 1.2 %collective-permute-done.4.refs_2_ = bf16[1,128,256]{2,1,0:T(8,128)(2,1)S(1)} collective-permute-done((bf16[1,128,256]{2,1,0:T(8,128)(2,1)S(1)}, bf16[1,128,256]{2,1,0:T(8,128)(2,1)S(1)}, u32[]{:S(2)}, u32[]{:S(2)}) %collective-permute-start.4) | collective-permute-done | bytes 65568 | tf_op jit(solution)/shard_map/ppermute | solution.py:395
  21.1 0.5 %collective-permute-done.3.refs_1_ = bf16[1,128,256]{2,1,0:T(8,128)(2,1)S(1)} collective-permute-done((bf16[1,128,256]{2,1,0:T(8,128)(2,1)S(1)}, bf16[1,128,256]{2,1,0:T(8,128)(2,1)S(1)}, u32[]{:S(2)}, u32[]{:S(2)}) %collective-permute-start.3) | collective-permute-done | bytes 65568 | tf_op jit(solution)/shard_map/ppermute | solution.py:395
  21.6 0.1 collective-permute-start.6
  21.7 0.0 copy-done
  21.7 0.0 copy-done.1
  21.7 0.0 copy-done.2
  21.7 1.2 %first_pair.1.refs_1_ = bf16[512,1024]{1,0:T(8,128)(2,1)S(1)} custom-call(bf16[4,128,256]{2,1,0:T(8,128)(2,1)S(1)} %bitcast.4, f32[512,512]{1,0:T(8,128)S(1)} %get-tuple-element.17.real_ref.refs_2_, f32[512,512]{1,0:T(8,128)S(1)} %get-tuple-element.18.imag_ref.refs_3_, bf16[512,1024]{1,0:T(8,128)(2,1)S(1)} %copy-done, bf16[4,256,256]{2,1,0:T(8,128)(2,1)S(1)} %copy-done.2, ...), custom_call_target="tpu_custom_call" | custom-call | flops 805306368 | bytes 3145728 | tf_op jit(solution)/shard_map/first_pair/pallas_call | solution.py:308
  23.0 0.2 collective-permute-done.6.refs_0_
  23.2 0.0 copy-done.3
  23.2 0.0 copy-done.4
  23.2 0.0 copy-done.5
  23.2 3.4 %second_pair.1 = (f32[1,512,512]{2,1,0:T(8,128)}, f32[1,512,512]{2,1,0:T(8,128)}, f32[1,512,512]{2,1,0:T(8,128)}) custom-call(bf16[4,128,256]{2,1,0:T(8,128)(2,1)S(1)} %collective-permute-done.6.refs_0_, bf16[512,1024]{1,0:T(8,128)(2,1)S(1)} %first_pair.1.refs_1_, f32[512,512]{1,0:T(8,128)S(1)} %get-tuple-element.17.real_ref.refs_2_, ...), custom_call_target="tpu_custom_call" | custom-call | flops 1342177280 | bytes 10485760 | tf_op jit(solution)/shard_map/second_pair/pallas_call | solution.py:375
  (2 shorter events, 0.1 us)
Async XLA Ops:
  0.6 9.2 %copy-start.6 = (bf16[1,512,1024]{2,1,0:T(8,128)(2,1)S(1)}, bf16[1,512,1024]{2,1,0:T(8,128)(2,1)}, u32[]{:S(2)}) copy-start(bf16[1,512,1024]{2,1,0:T(8,128)(2,1)} %param.17) | copy-start | bytes 3145732
  2.7 19.0 %copy-start = (bf16[512,1024]{1,0:T(8,128)(2,1)S(1)}, bf16[512,1024]{1,0:T(8,128)(2,1)}, u32[]{:S(2)}) copy-start(bf16[512,1024]{1,0:T(8,128)(2,1)} %constant.6.clone.row_ref.refs_4_) | copy-start | bytes 3145732
  2.7 19.0 %copy-start.1 = (bf16[4,256,256]{2,1,0:T(8,128)(2,1)S(1)}, bf16[4,256,256]{2,1,0:T(8,128)(2,1)}, u32[]{:S(2)}) copy-start(bf16[4,256,256]{2,1,0:T(8,128)(2,1)} %constant.8.clone.quadt_ref.refs_6_) | copy-start | bytes 1572868
  2.8 19.0 %copy-start.2 = (bf16[4,256,256]{2,1,0:T(8,128)(2,1)S(1)}, bf16[4,256,256]{2,1,0:T(8,128)(2,1)}, u32[]{:S(2)}) copy-start(bf16[4,256,256]{2,1,0:T(8,128)(2,1)} %constant.7.clone.quad_ref.refs_5_) | copy-start | bytes 1572868
  2.8 9.6 %collective-permute-start.2 = (bf16[128,256]{1,0:T(8,128)(2,1)S(1)}, bf16[128,256]{1,0:T(8,128)(2,1)S(1)}, u32[]{:S(2)}, u32[]{:S(2)}) collective-permute-start(bf16[128,256]{1,0:T(8,128)(2,1)S(1)} %project.1.refs_0_), channel_id=1, source_target_pairs={{0,2},{1,3},{2,0},{3,1},{4,6},{5,7},{6,4},{7,5},{8,10},{9,11},{10,... | collective-permute-start | bytes 196616 | tf_op jit(solution)/shard_map/ppermute | solution.py:395
  7.6 6.5 %collective-permute-start.1 = (bf16[128,256]{1,0:T(8,128)(2,1)S(1)}, bf16[128,256]{1,0:T(8,128)(2,1)S(1)}, u32[]{:S(2)}, u32[]{:S(2)}) collective-permute-start(bf16[128,256]{1,0:T(8,128)(2,1)S(1)} %project.1.refs_0_), channel_id=1, source_target_pairs={{0,3},{1,2},{2,1},{3,0},{4,7},{5,6},{6,5},{7,4},{8,11},{9,10},{10,... | collective-permute-start | bytes 196616 | tf_op jit(solution)/shard_map/ppermute | solution.py:395
  9.8 4.8 %collective-permute-start = (bf16[128,256]{1,0:T(8,128)(2,1)S(1)}, bf16[128,256]{1,0:T(8,128)(2,1)S(1)}, u32[]{:S(2)}, u32[]{:S(2)}) collective-permute-start(bf16[128,256]{1,0:T(8,128)(2,1)S(1)} %project.1.refs_0_), channel_id=1, source_target_pairs={{0,1},{1,0},{2,3},{3,2},{4,5},{5,4},{6,7},{7,6},{8,9},{9,8},{10,11... | collective-permute-start | bytes 196616 | tf_op jit(solution)/shard_map/ppermute | solution.py:395
  9.8 13.4 %copy-start.3 = (f32[1,512,512]{2,1,0:T(8,128)S(1)}, f32[1,512,512]{2,1,0:T(8,128)}, u32[]{:S(2)}) copy-start(f32[1,512,512]{2,1,0:T(8,128)} %refs_7_.1) | copy-start | bytes 3145732
  9.8 13.4 %copy-start.4 = (f32[1,512,512]{2,1,0:T(8,128)S(1)}, f32[1,512,512]{2,1,0:T(8,128)}, u32[]{:S(2)}) copy-start(f32[1,512,512]{2,1,0:T(8,128)} %refs_8_.1) | copy-start | bytes 3145732
  9.9 13.4 %copy-start.5 = (f32[1,512,512]{2,1,0:T(8,128)S(1)}, f32[1,512,512]{2,1,0:T(8,128)}, u32[]{:S(2)}) copy-start(f32[1,512,512]{2,1,0:T(8,128)} %refs_9_.1) | copy-start | bytes 3145732
  14.7 5.2 %collective-permute-start.5 = (bf16[1,128,256]{2,1,0:T(8,128)(2,1)S(1)}, bf16[1,128,256]{2,1,0:T(8,128)(2,1)S(1)}, u32[]{:S(2)}, u32[]{:S(2)}) collective-permute-start(bf16[1,128,256]{2,1,0:T(8,128)(2,1)S(1)} %bitcast.5), channel_id=1, source_target_pairs={{0,24},{4,28},{8,16},{12,20},{16,8},{20,12},{24,0},{28,4},{1,25},{... | collective-permute-start | bytes 196616 | tf_op jit(solution)/shard_map/ppermute | solution.py:395
  16.8 4.3 %collective-permute-start.4 = (bf16[1,128,256]{2,1,0:T(8,128)(2,1)S(1)}, bf16[1,128,256]{2,1,0:T(8,128)(2,1)S(1)}, u32[]{:S(2)}, u32[]{:S(2)}) collective-permute-start(bf16[1,128,256]{2,1,0:T(8,128)(2,1)S(1)} %bitcast.6), channel_id=1, source_target_pairs={{0,16},{4,20},{8,24},{12,28},{16,0},{20,4},{24,8},{28,12},{1,17},{... | collective-permute-start | bytes 196616 | tf_op jit(solution)/shard_map/ppermute | solution.py:395
  17.3 4.3 %collective-permute-start.3 = (bf16[1,128,256]{2,1,0:T(8,128)(2,1)S(1)}, bf16[1,128,256]{2,1,0:T(8,128)(2,1)S(1)}, u32[]{:S(2)}, u32[]{:S(2)}) collective-permute-start(bf16[1,128,256]{2,1,0:T(8,128)(2,1)S(1)} %bitcast.7), channel_id=1, source_target_pairs={{0,8},{4,12},{8,0},{12,4},{16,24},{20,28},{24,16},{28,20},{1,9},{5... | collective-permute-start | bytes 196616 | tf_op jit(solution)/shard_map/ppermute | solution.py:395
  21.6 1.6 %collective-permute-start.6 = (bf16[4,128,256]{2,1,0:T(8,128)(2,1)S(1)}, bf16[4,128,256]{2,1,0:T(8,128)(2,1)S(1)}, u32[]{:S(2)}, u32[]{:S(2)}) collective-permute-start(bf16[4,128,256]{2,1,0:T(8,128)(2,1)S(1)} %bitcast.3), channel_id=1, source_target_pairs={{0,4},{4,0},{8,12},{12,8},{16,20},{20,16},{24,28},{28,24},{1,5},{5... | collective-permute-start | bytes 786440 | tf_op jit(solution)/shard_map/ppermute | solution.py:395

commit v5 on v4

--- a/solution.py
+++ b/solution.py
@@ -395,6 +395,11 @@
     return lax.ppermute(value, axis, [(i, i ^ offset) for i in range(lax.axis_size(axis))])
 
 
+def swaps(value, axis, low_bit, count):
+    order = sorted(range(1, count), key=lambda k: (k & (k - 1) == 0 and k > 1, k))
+    return {k: swap(value, axis, k << low_bit) for k in order}
+
+
 def assemble_kernel(low_bit, bits, *refs):
     mine = (lax.axis_index("mic") >> low_bit) & ((1 << bits) - 1)
     for k, ref in enumerate(refs[:-1]):
@@ -402,7 +407,7 @@
 
 
 def gather_group(value, low_bit, bits):
-    got = [swap(value, "mic", k << low_bit) for k in range(1, 1 << bits)]
+    got = swaps(value, "mic", low_bit, 1 << bits)
     vmem = pl.BlockSpec(memory_space=pltpu.VMEM)
     out = pl.pallas_call(
         lambda *refs: assemble_kernel(low_bit, bits, *refs),
@@ -411,7 +416,7 @@
         out_specs=vmem,
         compiler_params=pltpu.CompilerParams(vmem_limit_bytes=4 << 20),
         name="assemble",
-    )(value, *got)
+    )(value, *(got[k] for k in range(1, 1 << bits)))
     return out.reshape((-1,) + value.shape[1:])
 
 
@@ -423,7 +428,7 @@
     row, quad, quad_t = constants(box, edge)
 
     part = project(map_slabs, slot_slab, orient_index, slab_lo, slab_hi, rows)
-    got = [swap(part, "proj", k) for k in sorted(range(1, lax.axis_size("proj")), key=lambda k: (k & (k - 1) == 0 and k > 1, k))]
+    got = list(swaps(part, "proj", 0, lax.axis_size("proj")).values())
     tile, _ = lax.optimization_barrier((tile_spectrum[0], part))
     th_real, th_imag = hermitian(tile)
     got, th_real, th_imag = lax.optimization_barrier((got, th_real, th_imag))

time: 26.7 us -> 26.8 us (level)
  waiting for transfers between devices: 5.92 us -> 6.66 us
  starting transfers between devices: 10.7 us -> 9.99 us
    ppermute x7, waiting for transfers between devices: 5.92 us -> 6.66 us  [swap(): lax.ppermute(value, axis, [(i, i ^ offset) for i in range(lax.axis_size(a...]
    ppermute x7, starting transfers between devices: 10.7 us -> 9.99 us  [swap(): lax.ppermute(value, axis, [(i, i ^ offset) for i in range(lax.axis_size(a...]
where the time goes in v5:
time: 26.8 us; the launch traced here: 26.7 us
  starting transfers between devices  9.99 us (37%)
  Pallas kernels  9.28 us (35%)
  waiting for transfers between devices  6.66 us (25%)
  between operations  0.75 us (3%)
    ppermute x7, starting transfers between devices, swap(): lax.ppermute(value, axis, [(i, i ^ offset) for i in range(lax.axis_size(a...  9.99 us
    ppermute x7, waiting for transfers between devices, swap(): lax.ppermute(value, axis, [(i, i ^ offset) for i in range(lax.axis_size(a...  6.66 us
    pallas_call x1, Pallas kernels, second_pair(): pl.pallas_call(lambda *refs: second_kernel(block, *refs), out_shape=[jax....  3.45 us
    pallas_call x1, Pallas kernels, hermitian(): pl.pallas_call(hermitian_kernel, out_shape=[jax.ShapeDtypeStruct((edge, e...  2.45 us
    pallas_call x1, Pallas kernels, project(): pl.pallas_call(lambda *refs: project_kernel(rows, window, *refs), out_sha...  2.08 us
    pallas_call x1, Pallas kernels, first_pair(): pl.pallas_call(first_kernel, out_shape=jax.ShapeDtypeStruct((edge, 2 * ed...  1.24 us
  transfers between devices with their start and end apart: 7, of which 6 were waited for; matrix products, arithmetic and copies ran while one was open for 0% of the time, Pallas kernels for 14%

profile of v5, /device:TPU:0, one launch (start us, length us, event | category | flops | bytes accessed | tf_op | source)
XLA Modules:
  0.0 26.7 jit_solution(1995775213955387672)
XLA Ops:
  0.6 0.0 copy-start.6
  0.6 2.1 %project.1.refs_0_ = bf16[128,256]{1,0:T(8,128)(2,1)S(1)} custom-call(s32[5]{0:T(128)} %refs_0_.1, s32[4]{0:T(128)} %refs_1_.1, s32[4]{0:T(128)} %refs_2_.1, s32[4]{0:T(128)} %refs_3_.1, bf16[5,8,256,256]{3,2,1,0:T(8,128)(2,1)} %refs_4_.2), custom_call_target="tpu_custom_call" | custom-call | tf_op jit(solution)/shard_map/project/pallas_call | solution.py:155
  2.7 0.0 copy-start
  2.7 0.0 copy-start.1
  2.8 0.0 copy-start.2
  2.8 4.6 %collective-permute-start.2 = (bf16[128,256]{1,0:T(8,128)(2,1)S(1)}, bf16[128,256]{1,0:T(8,128)(2,1)S(1)}, u32[]{:S(2)}, u32[]{:S(2)}) collective-permute-start(bf16[128,256]{1,0:T(8,128)(2,1)S(1)} %project.1.refs_0_), channel_id=1, source_target_pairs={{0,2},{1,3},{2,0},{3,1},{4,6},{5,7},{6,4},{7,5},{8,10},{9,11},{10,... | collective-permute-start | bytes 196616 | tf_op jit(solution)/shard_map/ppermute | solution.py:395
  7.4 1.2 %collective-permute-start.1 = (bf16[128,256]{1,0:T(8,128)(2,1)S(1)}, bf16[128,256]{1,0:T(8,128)(2,1)S(1)}, u32[]{:S(2)}, u32[]{:S(2)}) collective-permute-start(bf16[128,256]{1,0:T(8,128)(2,1)S(1)} %project.1.refs_0_), channel_id=1, source_target_pairs={{0,3},{1,2},{2,1},{3,0},{4,7},{5,6},{6,5},{7,4},{8,11},{9,10},{10,... | collective-permute-start | bytes 196616 | tf_op jit(solution)/shard_map/ppermute | solution.py:395
  8.5 0.5 %collective-permute-start = (bf16[128,256]{1,0:T(8,128)(2,1)S(1)}, bf16[128,256]{1,0:T(8,128)(2,1)S(1)}, u32[]{:S(2)}, u32[]{:S(2)}) collective-permute-start(bf16[128,256]{1,0:T(8,128)(2,1)S(1)} %project.1.refs_0_), channel_id=1, source_target_pairs={{0,1},{1,0},{2,3},{3,2},{4,5},{5,4},{6,7},{7,6},{8,9},{9,8},{10,11... | collective-permute-start | bytes 196616 | tf_op jit(solution)/shard_map/ppermute | solution.py:395
  9.0 0.0 copy-done.6
  9.0 0.0 copy-start.3
  9.0 0.0 copy-start.4
  9.0 0.0 copy-start.5
  9.0 2.4 %hermitian.1 = (f32[512,512]{1,0:T(8,128)S(1)}, f32[512,512]{1,0:T(8,128)S(1)}) custom-call(bf16[512,1024]{1,0:T(8,128)(2,1)S(1)} %bitcast.9), custom_call_target="tpu_custom_call" | custom-call | flops 2147483648 | bytes 3145728 | tf_op jit(solution)/shard_map/hermitian/pallas_call | solution.py:223
  11.5 0.0 collective-permute-done.2.refs_3_
  11.5 2.2 %collective-permute-done.1.refs_2_ = bf16[128,256]{1,0:T(8,128)(2,1)S(1)} collective-permute-done((bf16[128,256]{1,0:T(8,128)(2,1)S(1)}, bf16[128,256]{1,0:T(8,128)(2,1)S(1)}, u32[]{:S(2)}, u32[]{:S(2)}) %collective-permute-start.1) | collective-permute-done | bytes 65568 | tf_op jit(solution)/shard_map/ppermute | solution.py:395
  13.7 0.1 collective-permute-done.refs_1_
  13.8 3.0 %collective-permute-start.5 = (bf16[1,128,256]{2,1,0:T(8,128)(2,1)S(1)}, bf16[1,128,256]{2,1,0:T(8,128)(2,1)S(1)}, u32[]{:S(2)}, u32[]{:S(2)}) collective-permute-start(bf16[1,128,256]{2,1,0:T(8,128)(2,1)S(1)} %bitcast.5), channel_id=1, source_target_pairs={{0,24},{4,28},{8,16},{12,20},{16,8},{20,12},{24,0},{28,4},{1,25},{... | collective-permute-start | bytes 196616 | tf_op jit(solution)/shard_map/ppermute | solution.py:395
  16.9 0.5 %collective-permute-start.4 = (bf16[1,128,256]{2,1,0:T(8,128)(2,1)S(1)}, bf16[1,128,256]{2,1,0:T(8,128)(2,1)S(1)}, u32[]{:S(2)}, u32[]{:S(2)}) collective-permute-start(bf16[1,128,256]{2,1,0:T(8,128)(2,1)S(1)} %bitcast.6), channel_id=1, source_target_pairs={{0,16},{4,20},{8,24},{12,28},{16,0},{20,4},{24,8},{28,12},{1,17},{... | collective-permute-start | bytes 196616 | tf_op jit(solution)/shard_map/ppermute | solution.py:395
  17.4 0.1 collective-permute-start.3
  17.5 1.7 %collective-permute-done.5.refs_3_ = bf16[1,128,256]{2,1,0:T(8,128)(2,1)S(1)} collective-permute-done((bf16[1,128,256]{2,1,0:T(8,128)(2,1)S(1)}, bf16[1,128,256]{2,1,0:T(8,128)(2,1)S(1)}, u32[]{:S(2)}, u32[]{:S(2)}) %collective-permute-start.5) | collective-permute-done | bytes 65568 | tf_op jit(solution)/shard_map/ppermute | solution.py:395
  19.2 1.9 %collective-permute-done.4.refs_2_ = bf16[1,128,256]{2,1,0:T(8,128)(2,1)S(1)} collective-permute-done((bf16[1,128,256]{2,1,0:T(8,128)(2,1)S(1)}, bf16[1,128,256]{2,1,0:T(8,128)(2,1)S(1)}, u32[]{:S(2)}, u32[]{:S(2)}) %collective-permute-start.4) | collective-permute-done | bytes 65568 | tf_op jit(solution)/shard_map/ppermute | solution.py:395
  21.1 0.5 %collective-permute-done.3.refs_1_ = bf16[1,128,256]{2,1,0:T(8,128)(2,1)S(1)} collective-permute-done((bf16[1,128,256]{2,1,0:T(8,128)(2,1)S(1)}, bf16[1,128,256]{2,1,0:T(8,128)(2,1)S(1)}, u32[]{:S(2)}, u32[]{:S(2)}) %collective-permute-start.3) | collective-permute-done | bytes 65568 | tf_op jit(solution)/shard_map/ppermute | solution.py:395
  21.6 0.1 collective-permute-start.6
  21.7 0.0 copy-done
  21.7 0.0 copy-done.1
  21.7 0.0 copy-done.2
  21.8 1.2 %first_pair.1.refs_1_ = bf16[512,1024]{1,0:T(8,128)(2,1)S(1)} custom-call(bf16[4,128,256]{2,1,0:T(8,128)(2,1)S(1)} %bitcast.4, f32[512,512]{1,0:T(8,128)S(1)} %get-tuple-element.17.real_ref.refs_2_, f32[512,512]{1,0:T(8,128)S(1)} %get-tuple-element.18.imag_ref.refs_3_, bf16[512,1024]{1,0:T(8,128)(2,1)S(1)} %copy-done, bf16[4,256,256]{2,1,0:T(8,128)(2,1)S(1)} %copy-done.2, ...), custom_call_target="tpu_custom_call" | custom-call | flops 805306368 | bytes 3145728 | tf_op jit(solution)/shard_map/first_pair/pallas_call | solution.py:308
  23.0 0.2 collective-permute-done.6.refs_0_
  23.3 0.0 copy-done.3
  23.3 0.0 copy-done.4
  23.3 0.0 copy-done.5
  23.3 3.4 %second_pair.1 = (f32[1,512,512]{2,1,0:T(8,128)}, f32[1,512,512]{2,1,0:T(8,128)}, f32[1,512,512]{2,1,0:T(8,128)}) custom-call(bf16[4,128,256]{2,1,0:T(8,128)(2,1)S(1)} %collective-permute-done.6.refs_0_, bf16[512,1024]{1,0:T(8,128)(2,1)S(1)} %first_pair.1.refs_1_, f32[512,512]{1,0:T(8,128)S(1)} %get-tuple-element.17.real_ref.refs_2_, ...), custom_call_target="tpu_custom_call" | custom-call | flops 1342177280 | bytes 10485760 | tf_op jit(solution)/shard_map/second_pair/pallas_call | solution.py:375
  (2 shorter events, 0.1 us)
Async XLA Ops:
  0.6 8.4 %copy-start.6 = (bf16[1,512,1024]{2,1,0:T(8,128)(2,1)S(1)}, bf16[1,512,1024]{2,1,0:T(8,128)(2,1)}, u32[]{:S(2)}) copy-start(bf16[1,512,1024]{2,1,0:T(8,128)(2,1)} %param.17) | copy-start | bytes 3145732
  2.7 19.0 %copy-start = (bf16[512,1024]{1,0:T(8,128)(2,1)S(1)}, bf16[512,1024]{1,0:T(8,128)(2,1)}, u32[]{:S(2)}) copy-start(bf16[512,1024]{1,0:T(8,128)(2,1)} %constant.6.clone.row_ref.refs_4_) | copy-start | bytes 3145732
  2.7 19.0 %copy-start.1 = (bf16[4,256,256]{2,1,0:T(8,128)(2,1)S(1)}, bf16[4,256,256]{2,1,0:T(8,128)(2,1)}, u32[]{:S(2)}) copy-start(bf16[4,256,256]{2,1,0:T(8,128)(2,1)} %constant.8.clone.quadt_ref.refs_6_) | copy-start | bytes 1572868
  2.8 19.0 %copy-start.2 = (bf16[4,256,256]{2,1,0:T(8,128)(2,1)S(1)}, bf16[4,256,256]{2,1,0:T(8,128)(2,1)}, u32[]{:S(2)}) copy-start(bf16[4,256,256]{2,1,0:T(8,128)(2,1)} %constant.7.clone.quad_ref.refs_5_) | copy-start | bytes 1572868
  2.8 8.7 %collective-permute-start.2 = (bf16[128,256]{1,0:T(8,128)(2,1)S(1)}, bf16[128,256]{1,0:T(8,128)(2,1)S(1)}, u32[]{:S(2)}, u32[]{:S(2)}) collective-permute-start(bf16[128,256]{1,0:T(8,128)(2,1)S(1)} %project.1.refs_0_), channel_id=1, source_target_pairs={{0,2},{1,3},{2,0},{3,1},{4,6},{5,7},{6,4},{7,5},{8,10},{9,11},{10,... | collective-permute-start | bytes 196616 | tf_op jit(solution)/shard_map/ppermute | solution.py:395
  7.4 6.3 %collective-permute-start.1 = (bf16[128,256]{1,0:T(8,128)(2,1)S(1)}, bf16[128,256]{1,0:T(8,128)(2,1)S(1)}, u32[]{:S(2)}, u32[]{:S(2)}) collective-permute-start(bf16[128,256]{1,0:T(8,128)(2,1)S(1)} %project.1.refs_0_), channel_id=1, source_target_pairs={{0,3},{1,2},{2,1},{3,0},{4,7},{5,6},{6,5},{7,4},{8,11},{9,10},{10,... | collective-permute-start | bytes 196616 | tf_op jit(solution)/shard_map/ppermute | solution.py:395
  8.5 5.3 %collective-permute-start = (bf16[128,256]{1,0:T(8,128)(2,1)S(1)}, bf16[128,256]{1,0:T(8,128)(2,1)S(1)}, u32[]{:S(2)}, u32[]{:S(2)}) collective-permute-start(bf16[128,256]{1,0:T(8,128)(2,1)S(1)} %project.1.refs_0_), channel_id=1, source_target_pairs={{0,1},{1,0},{2,3},{3,2},{4,5},{5,4},{6,7},{7,6},{8,9},{9,8},{10,11... | collective-permute-start | bytes 196616 | tf_op jit(solution)/shard_map/ppermute | solution.py:395
  9.0 14.2 %copy-start.3 = (f32[1,512,512]{2,1,0:T(8,128)S(1)}, f32[1,512,512]{2,1,0:T(8,128)}, u32[]{:S(2)}) copy-start(f32[1,512,512]{2,1,0:T(8,128)} %refs_7_.1) | copy-start | bytes 3145732
  9.0 14.2 %copy-start.4 = (f32[1,512,512]{2,1,0:T(8,128)S(1)}, f32[1,512,512]{2,1,0:T(8,128)}, u32[]{:S(2)}) copy-start(f32[1,512,512]{2,1,0:T(8,128)} %refs_8_.1) | copy-start | bytes 3145732
  9.0 14.2 %copy-start.5 = (f32[1,512,512]{2,1,0:T(8,128)S(1)}, f32[1,512,512]{2,1,0:T(8,128)}, u32[]{:S(2)}) copy-start(f32[1,512,512]{2,1,0:T(8,128)} %refs_9_.1) | copy-start | bytes 3145732
  13.8 5.4 %collective-permute-start.5 = (bf16[1,128,256]{2,1,0:T(8,128)(2,1)S(1)}, bf16[1,128,256]{2,1,0:T(8,128)(2,1)S(1)}, u32[]{:S(2)}, u32[]{:S(2)}) collective-permute-start(bf16[1,128,256]{2,1,0:T(8,128)(2,1)S(1)} %bitcast.5), channel_id=1, source_target_pairs={{0,24},{4,28},{8,16},{12,20},{16,8},{20,12},{24,0},{28,4},{1,25},{... | collective-permute-start | bytes 196616 | tf_op jit(solution)/shard_map/ppermute | solution.py:395
  16.9 4.3 %collective-permute-start.4 = (bf16[1,128,256]{2,1,0:T(8,128)(2,1)S(1)}, bf16[1,128,256]{2,1,0:T(8,128)(2,1)S(1)}, u32[]{:S(2)}, u32[]{:S(2)}) collective-permute-start(bf16[1,128,256]{2,1,0:T(8,128)(2,1)S(1)} %bitcast.6), channel_id=1, source_target_pairs={{0,16},{4,20},{8,24},{12,28},{16,0},{20,4},{24,8},{28,12},{1,17},{... | collective-permute-start | bytes 196616 | tf_op jit(solution)/shard_map/ppermute | solution.py:395
  17.4 4.3 %collective-permute-start.3 = (bf16[1,128,256]{2,1,0:T(8,128)(2,1)S(1)}, bf16[1,128,256]{2,1,0:T(8,128)(2,1)S(1)}, u32[]{:S(2)}, u32[]{:S(2)}) collective-permute-start(bf16[1,128,256]{2,1,0:T(8,128)(2,1)S(1)} %bitcast.7), channel_id=1, source_target_pairs={{0,8},{4,12},{8,0},{12,4},{16,24},{20,28},{24,16},{28,20},{1,9},{5... | collective-permute-start | bytes 196616 | tf_op jit(solution)/shard_map/ppermute | solution.py:395
  21.6 1.6 %collective-permute-start.6 = (bf16[4,128,256]{2,1,0:T(8,128)(2,1)S(1)}, bf16[4,128,256]{2,1,0:T(8,128)(2,1)S(1)}, u32[]{:S(2)}, u32[]{:S(2)}) collective-permute-start(bf16[4,128,256]{2,1,0:T(8,128)(2,1)S(1)} %bitcast.3), channel_id=1, source_target_pairs={{0,4},{4,0},{8,12},{12,8},{16,20},{20,16},{24,28},{28,24},{1,5},{5... | collective-permute-start | bytes 786440 | tf_op jit(solution)/shard_map/ppermute | solution.py:395
